TPU v7x, 128 devices: a whole 4x4x4 slice. The times are simulated.
128 devices in a mesh: ctx: 8 (over x_hi, z), exp: 16 (over x_lo, y, core).
Axes of the slice: x: 4 (x_hi: 2, x_lo: 2; x = x_hi * 2 + x_lo), y: 4, z: 4, core: 2. Of those that a mesh axis runs over, the one named last changes fastest.
Arguments:
- queries: bfloat16 [16, 1024, 6144], P('exp', 'ctx'), may hold values from -140 to 140
- keys_values: bfloat16 [16, 1024, 2048], P('exp', 'ctx'), may hold values from -4.5 to 4.5
- doc_ids: int32 [16, 1024], P('exp', 'ctx'), may hold values from 0 to 15, never falling along the last dimension, each value on 1 to 512 neighbouring positions
- expert_ids: int32 [16, 1024, 1], P('exp', 'ctx'), may hold values from 0 to 15; in each aligned block of 128 rows (0 to 127, 128 to 255, ..., all dimensions but the last counted through in order) at most 10 rows name the same one
- gate_probs: float32 [16, 1024, 1], P('exp', 'ctx'), may hold values from 0.25 to 1
- w_gate: bfloat16 [16, 6144, 5376], P('exp', None, 'ctx'), may hold values from -0.078125 to 0.078125
- w_down: bfloat16 [16, 5376, 6144], P('exp', 'ctx'), may hold values from -0.078125 to 0.078125
Outputs:
- layer_out: bfloat16 [16, 1024, 6144], P('exp', 'ctx')
Inputs may be any that keep to these rules, and one draw needn't show every extreme that they name: `doc_ids`: document numbers never fall along a sequence; a document covers at most 512 positions and one covers exactly that many. `expert_ids`: within the 128 tokens of one device (aligned blocks of the flattened sequences), no expert is named more than 10 times, a bound that some block reaches.
All inputs are finite; a program needn't handle non-finite values.
Results may differ from a plain program's by a relative error of at most 0.01.
Values may be sent and summed in bfloat16 or wider, within the bound.
No kernel may reach another device: no remote copies, remote signals or barrier semaphores. Data moves between devices by JAX's collectives and lax.ppermute only.
A program may use at most 192 MiB of HBM per device.

v0:
```python
import math

import jax
import jax.numpy as jnp
from jax import lax
from jax.sharding import PartitionSpec as P

D = 6144
QUERY_HEADS = 48
KEY_VALUE_HEADS = 8
HEAD_WIDTH = 128
TOPK = 1
QUERY_PER_KEY = 6


def masked_scores(query_head_rows, key_block, query_docs, block_docs, query_places, block_places):
    scores = jnp.einsum(
        "qhgd,khd->hgqk", query_head_rows, key_block, preferred_element_type=jnp.float32
    ) * (1.0 / math.sqrt(HEAD_WIDTH))
    allowed = (query_docs[:, None] == block_docs[None, :]) & (
        block_places[None, :] <= query_places[:, None]
    )
    return jnp.where(allowed, scores, -1e30)


def on_device(queries, keys_values, doc_ids, expert_ids, gate_probs, w_gate, w_down):
    ctx_count = lax.axis_size("ctx")
    exp_count = lax.axis_size("exp")
    document_tokens = queries.shape[1]
    sequence_length = document_tokens * ctx_count
    every_key, docs_all = (
        lax.all_gather(keys_values, "ctx", axis=1, tiled=True),
        lax.all_gather(doc_ids, "ctx", axis=1, tiled=True),
    )
    query_head_rows = queries[0].reshape(
        document_tokens, KEY_VALUE_HEADS, QUERY_PER_KEY, HEAD_WIDTH
    )
    key_head_rows = every_key[0, :, : KEY_VALUE_HEADS * HEAD_WIDTH].reshape(
        sequence_length, KEY_VALUE_HEADS, HEAD_WIDTH
    )
    value_head_rows = every_key[0, :, KEY_VALUE_HEADS * HEAD_WIDTH :].reshape(
        sequence_length, KEY_VALUE_HEADS, HEAD_WIDTH
    )
    query_docs = doc_ids[0]
    key_docs = docs_all[0]
    query_places = lax.axis_index("ctx") * document_tokens + jnp.arange(
        document_tokens, dtype=jnp.int32
    )
    key_places = jnp.arange(sequence_length, dtype=jnp.int32)
    scores = masked_scores(
        query_head_rows, key_head_rows, query_docs, key_docs, query_places, key_places
    )
    row_max = jnp.max(scores, axis=-1, keepdims=True)
    weights = jnp.exp(scores - row_max)
    totals = jnp.sum(weights, axis=-1)
    blended = jnp.einsum(
        "hgqk,khd->qhgd",
        weights.astype(jnp.bfloat16),
        value_head_rows,
        preferred_element_type=jnp.float32,
    )
    blended = blended / jnp.transpose(totals, (2, 0, 1))[..., None]
    attended = blended.reshape(document_tokens, QUERY_HEADS * HEAD_WIDTH).astype(jnp.bfloat16)
    widened = attended.astype(jnp.float32)
    centered = widened - jnp.mean(widened, axis=-1, keepdims=True)
    variance = jnp.mean(centered * centered, axis=-1, keepdims=True)
    normed = (centered * lax.rsqrt(variance + 1e-05)).astype(jnp.bfloat16)
    experts_total = exp_count * w_gate.shape[0]
    capacity = 5 * document_tokens * TOPK // (4 * experts_total)
    routed = expert_ids[0].reshape(document_tokens * TOPK)
    expert_hot = (routed[:, None] == jnp.arange(experts_total, dtype=jnp.int32)[None, :]).astype(
        jnp.int32
    )
    slot_ranks = jnp.sum((jnp.cumsum(expert_hot, axis=0) - 1) * expert_hot, axis=1)
    slot_index = routed * capacity + slot_ranks
    dispatch = (
        jnp.arange(experts_total * capacity, dtype=jnp.int32)[:, None] == slot_index[None, :]
    ).astype(jnp.bfloat16)
    token_dispatch = jnp.sum(
        dispatch.reshape(experts_total * capacity, document_tokens, TOPK), axis=2
    )
    outgoing = jnp.dot(token_dispatch, normed, preferred_element_type=jnp.float32).astype(
        jnp.bfloat16
    )
    outgoing = outgoing.reshape(experts_total, capacity, D)
    gate_local = w_gate[0]
    down_local = w_down[0]
    copies = jnp.broadcast_to(outgoing[None], (ctx_count, experts_total, capacity, D))
    copies = copies.reshape(ctx_count * experts_total, capacity, D)
    arrived = lax.all_to_all(copies, ("ctx", "exp"), split_axis=0, concat_axis=0, tiled=True)
    source_count = arrived.shape[0]
    item_count = arrived.shape[1]
    flat_rows = arrived.reshape(source_count * item_count, D)
    hidden = jax.nn.silu(jnp.dot(flat_rows, gate_local, preferred_element_type=jnp.float32)).astype(
        jnp.bfloat16
    )
    partial_value = jnp.dot(hidden, down_local, preferred_element_type=jnp.float32).astype(
        jnp.bfloat16
    )
    partial_value = partial_value.reshape(source_count, item_count, D)
    returned = lax.all_to_all(
        partial_value, ("ctx", "exp"), split_axis=0, concat_axis=0, tiled=True
    )
    returned = returned.reshape(ctx_count, experts_total, capacity, D).astype(jnp.float32)
    expert_out = jnp.sum(returned, axis=0).astype(jnp.bfloat16)
    per_pair = jnp.einsum(
        "sp,sd->pd",
        dispatch,
        expert_out.reshape(experts_total * capacity, D),
        preferred_element_type=jnp.float32,
    )
    per_pair = per_pair.reshape(document_tokens, TOPK, D)
    combined = widened + jnp.sum(gate_probs[0][:, :, None] * per_pair, axis=1)
    return combined.astype(jnp.bfloat16)[None]


def solution(mesh):
    return jax.shard_map(
        on_device,
        mesh=mesh,
        in_specs=(
            P("exp", "ctx", None),
            P("exp", "ctx", None),
            P("exp", "ctx"),
            P("exp", "ctx", None),
            P("exp", "ctx", None),
            P("exp", None, "ctx"),
            P("exp", "ctx", None),
        ),
        out_specs=P("exp", "ctx", None),
        check_vma=False,
    )
```

profile of v0, /device:TPU:36, one launch (start us, length us, event | category | flops | bytes accessed | tf_op | source)
XLA Modules:
  0.0 936.7 jit_solution(11070336287133294352)
XLA Ops:
  6.5 2.1 copy.12
  8.6 1.9 copy.13
  10.8 18.1 %all_gather.6 = s32[1,1024]{1,0:T(1,128)S(1)} all-gather(s32[1,128]{1,0:T(1,128)S(1)} %copy-done.2), channel_id=1, replica_groups=mesh['ctx'=8,'exp'=16] {'ctx'}, dimensions={1}, use_global_device_ids=true | all-gather | bytes 4608 | tf_op jit(solution)/shard_map/all_gather | solution.py:33
  29.3 52.3 %all-gather.2.cloned.1.call-done = bf16[1,1024,2048]{1,2,0:T(8,128)(2,1)} async-done(((bf16[1,128,2048]{1,2,0:T(8,128)(2,1)}), bf16[1,1024,2048]{1,2,0:T(8,128)(2,1)}) %all-gather.2.cloned.1.call-update) | async-done | bytes 4194320 | tf_op jit(solution)/shard_map/all_gather | solution.py:32
  81.6 2.7 fusion.23
  84.3 10.3 %fusion.2 = (f32[8,6,128]{2,1,0:T(8,128)S(1)}, f32[8,1024,128,6]{2,1,3,0:T(8,128)}) fusion(pred[128,1024]{0,1:T(8,128)(4,1)S(1)} %fusion.17, bf16[1024,8,128,1]{0,2,3,1:T(8,128)(2,1)S(1)} %bitcast.58, bf16[128,8,6,128]{0,3,2,1:T(8,128)(2,1)S(1)} %bitcast.59), kind=kOutput, calls=%fused_computation.5 | convolution fusion | flops 1629480960 | bytes 28991488 | tf_op jit(solution)/shard_map/qhgd,khd->hgqk/dot_general | solution.py:17
  94.6 11.0 %fusion = f32[8,6,128]{2,1,0:T(8,128)S(1)} fusion(f32[8,1024,128,6]{2,1,3,0:T(8,128)} %get-tuple-element.8, f32[8,6,128]{2,1,0:T(8,128)S(1)} %get-tuple-element.7, pred[128,1024]{0,1:T(8,128)(4,1)S(1)} %fusion.17), kind=kLoop, calls=%fused_computation.3 | loop fusion | flops 25159680 | bytes 25346048 | tf_op jit(solution)/shard_map/reduce_sum | solution.py:55
  105.6 11.5 %convert_reduce_fusion = (f32[128]{0:T(128)S(1)}, bf16[128,8,6,128]{0,3,2,1:T(8,128)(2,1)S(1)}) fusion(f32[128,8,6]{0,2,1:T(8,128)S(1)} %bitcast.62, bf16[1024,8,128,1]{0,2,3,1:T(8,128)(2,1)S(1)} %bitcast.61, f32[8,1024,128,6]{2,1,3,0:T(8,128)} %get-tuple-element.8, f32[8,6,128]{2,1,0:T(8,128)S(1)} %get-tuple-element.7, pred[128,1024]{0,1:T(8,128)(4,1)S(1)} %fusion.17), kind=kOutput, calls=%fused_computation.21 | convolution fusion | flops 1638924160 | bytes 29016576 | tf_op jit(solution)/shard_map/hgqk,khd->qhgd/dot_general | solution.py:56
  117.1 0.8 multiply_reduce_fusion
  117.9 0.5 multiply_convert_fusion.1
  118.4 0.7 convolution_convert_fusion.1
  119.1 2.4 broadcast_in_dim.14
  121.5 5.5 broadcast_in_dim.15
  127.1 296.8 %all_to_all.10 = bf16[128,10,6144]{2,1,0:T(8,128)(2,1)} all-to-all(bf16[128,10,6144]{2,1,0:T(8,128)(2,1)S(1)} %bitcast.56), channel_id=1, replica_groups=mesh['ctx'=8,'exp'=16] {'ctx','exp'}, dimensions={0} | all-to-all | bytes 31457280 | tf_op jit(solution)/shard_map/all_to_all | solution.py:90
  423.9 26.3 %reshape.97 = bf16[1280,6144]{1,0:T(8,128)(2,1)} reshape(bf16[128,10,6144]{2,1,0:T(8,128)(2,1)} %all_to_all.10) | data formatting | bytes 31457280 | tf_op jit(solution)/shard_map/reshape | solution.py:93
  450.3 16.4 %multiply_convert_fusion = bf16[1280,672]{0,1:T(8,128)(2,1)S(1)} fusion(bf16[1280,6144]{1,0:T(8,128)(2,1)} %reshape.97, bf16[1,6144,672]{1,2,0:T(8,128)(2,1)} %param.12), kind=kOutput, calls=%fused_computation.16 | convolution fusion | flops 10573946880 | bytes 25706496 | tf_op jit(solution)/shard_map/dot_general | solution.py:94
  466.7 18.3 %convolution_convert_fusion = bf16[1280,6144]{1,0:T(8,128)(2,1)} fusion(bf16[1280,672]{0,1:T(8,128)(2,1)S(1)} %multiply_convert_fusion, bf16[1,672,6144]{2,1,0:T(8,128)(2,1)} %param.13), kind=kOutput, calls=%fused_computation.2 | convolution fusion | flops 10577510400 | bytes 25706496 | tf_op jit(solution)/shard_map/dot_general | solution.py:97
  485.0 25.9 %reshape.98 = bf16[128,10,6144]{2,1,0:T(8,128)(2,1)} reshape(bf16[1280,6144]{1,0:T(8,128)(2,1)} %convolution_convert_fusion) | data formatting | bytes 31457280 | tf_op jit(solution)/shard_map/reshape | solution.py:100
  510.9 13.9 %all-to-all-start.1 = ((bf16[128,10,6144]{2,1,0:T(8,128)(2,1)}), bf16[128,10,6144]{2,1,0:T(8,128)(2,1)}, u32[]{:S(2)}, u32[]{:S(2)}) async-start(bf16[128,10,6144]{2,1,0:T(8,128)(2,1)} %reshape.98), calls=%async_computation.1 | async-start | bytes 50331648 | tf_op jit(solution)/shard_map/all_to_all | solution.py:101
  524.7 2.0 copy.17
  526.7 379.4 %all-to-all-done.1 = bf16[128,10,6144]{2,1,0:T(8,128)(2,1)} async-done(((bf16[128,10,6144]{2,1,0:T(8,128)(2,1)}), bf16[128,10,6144]{2,1,0:T(8,128)(2,1)}, u32[]{:S(2)}, u32[]{:S(2)}) %all-to-all-start.1) | async-done | bytes 15728672 | tf_op jit(solution)/shard_map/all_to_all | solution.py:101
  906.2 15.9 %reduce_sum.60 = bf16[16,10,6144]{2,1,0:T(8,128)(2,1)} reduce(bf16[8,16,10,6144]{3,2,1,0:T(8,128)(2,1)} %bitcast.18, bf16[]{:T(256)} %constant.37.clone.1), dimensions={0}, to_apply=%region_6.7 | reduce | flops 6881280 | bytes 17694722 | tf_op jit(solution)/shard_map/reduce_sum | solution.py:105
  922.0 4.5 reshape.100
  926.5 3.3 fusion.11
  (18 shorter events, 0.7 us)
Async XLA Ops:
  6.5 4.0 copy-start.1
  6.5 4.3 copy-start.2
  6.5 75.1 %all-gather.2.cloned.1.call-start = ((), (), s32[]{:S(2)}) async-start(), calls=%async_computation.2 | async-start | bytes 4718592 | tf_op jit(solution)/shard_map/all_gather | solution.py:32
  510.9 395.3 %all-to-all-start.1 = ((bf16[128,10,6144]{2,1,0:T(8,128)(2,1)}), bf16[128,10,6144]{2,1,0:T(8,128)(2,1)}, u32[]{:S(2)}, u32[]{:S(2)}) async-start(bf16[128,10,6144]{2,1,0:T(8,128)(2,1)} %reshape.98), calls=%async_computation.1 | async-start | bytes 50331648 | tf_op jit(solution)/shard_map/all_to_all | solution.py:101
  922.0 4.5 copy-start
  922.0 4.5 copy-start.3
Sparse Core Ops, SparseCore 0:
  9.5 72.0 all-gather.1
where the time goes:
time: 939 us; the launch traced here: 937 us
  waiting for transfers between devices  432 us (46%)
  blocking collectives  315 us (34%)
  local copies, waits for them, and re-layouts  73.3 us (8%)
  matrix products  60.5 us (6%)
  other arithmetic  28.9 us (3%)
  starting transfers between devices  13.9 us (1%)
  between operations  13.5 us (1%)
    all_to_all x1, waiting for transfers between devices, on_device(): lax.all_to_all(partial_value, ('ctx', 'exp'), split_axis=0, concat_axis=0...  379 us
    all_to_all x1, blocking collectives, on_device(): lax.all_to_all(copies, ('ctx', 'exp'), split_axis=0, concat_axis=0, tiled...  297 us
    all_gather x1, waiting for transfers between devices, on_device(): lax.all_gather(keys_values, 'ctx', axis=1, tiled=True)  52.3 us
    reshape x1, local copies, waits for them, and re-layouts, on_device(): flat_rows = arrived.reshape(source_count * item_count, D)  26.3 us
    reshape x1, local copies, waits for them, and re-layouts, on_device(): partial_value = partial_value.reshape(source_count, item_count, D)  25.9 us
  transfers between devices with their start and end apart: 2, of which 2 were waited for; matrix products, arithmetic and copies ran while one was open for 0% of the time, Pallas kernels for 0%

commit v1 on v0

v1 whole, which is shorter than its diff:
```python
import math

import jax
import jax.numpy as jnp
from jax import lax
from jax.experimental import pallas as pl
from jax.experimental.pallas import tpu as pltpu
from jax.sharding import Mesh, PartitionSpec as P

D = 6144
HALF = D // 2
TOK = 128
KV_HEADS = 8
GROUP = 6
HW = 128
GW = GROUP * HW
WINDOW = 5
EXPERTS = 16
CAP = 10
MAIN = 8
FOLD = 4
UNIT = 672
PACK_ROWS = EXPERTS * MAIN
BLOCK_ROWS = EXPERTS * CAP
PIECES = (3072, 2048, 1024)
UNITS = (224, 112, 336)
VMEM = 50 * 1024 * 1024
PLANE = ("xl", "y", "xh")
HINT = pl.CostEstimate(flops=10**6, bytes_accessed=10**5, transcendentals=0)
BF = jnp.bfloat16
F32 = jnp.float32


def iota(shape, axis):
    return lax.broadcasted_iota(jnp.int32, shape, axis)


def dot(a, b):
    return jnp.dot(a, b, preferred_element_type=F32)


def dot_t(a, b):
    return lax.dot_general(a, b, (((1,), (1,)), ((), ())), preferred_element_type=F32)


def attend_kernel(place_ref, doc_ref, ecol_ref, erow_ref, q_ref, *refs):
    k_refs = refs[:WINDOW]
    v_refs = refs[WINDOW : 2 * WINDOW]
    d_refs = refs[2 * WINDOW : 3 * WINDOW]
    att_ref, send, bias, keys, values, held, scores, weights, totals = refs[3 * WINDOW :]
    head = pl.program_id(0)

    @pl.when(head == 0)
    def _():
        place = place_ref[0]
        mine = doc_ref[...]
        for n in range(WINDOW):
            same = mine == d_refs[n][...].astype(F32)
            if n == 0:
                ok = same & (iota((TOK, TOK), 1) <= iota((TOK, TOK), 0))
            else:
                ok = same & (iota((TOK, TOK), 0) * 0 + place >= n)
            bias[:, n * TOK : (n + 1) * TOK] = jnp.where(ok, 0.0, -1e30)

    for n in range(WINDOW):
        keys[n * TOK : (n + 1) * TOK, :] = k_refs[n][...]
        values[n * TOK : (n + 1) * TOK, :] = v_refs[n][...]
    stacked = jnp.concatenate([q_ref[:, i * HW : (i + 1) * HW] for i in range(GROUP)], axis=0)
    scores[...] = dot_t(stacked, keys[...])
    for i in range(GROUP):
        rows = slice(i * TOK, (i + 1) * TOK)
        s = scores[rows, :] * (math.log2(math.e) / math.sqrt(HW)) + bias[...]
        w = jnp.exp2(s - jnp.max(s, axis=1, keepdims=True))
        totals[rows, :] = jnp.sum(w, axis=1, keepdims=True)
        weights[rows, :] = w.astype(BF)
    blended = (dot(weights[...], values[...]) / totals[...]).astype(BF)
    for i in range(GROUP):
        o = blended[i * TOK : (i + 1) * TOK]
        att_ref[:, i * HW : (i + 1) * HW] = o
        held[head, :, i * HW : (i + 1) * HW] = o

    @pl.when(head == KV_HEADS - 1)
    def _():
        total = jnp.zeros((TOK, 1), F32)
        for g in range(KV_HEADS):
            total += jnp.sum(held[g].astype(F32), axis=1, keepdims=True)
        mean = total * (1.0 / D)
        square = jnp.zeros((TOK, 1), F32)
        for g in range(KV_HEADS):
            c = held[g].astype(F32) - mean
            square += jnp.sum(c * c, axis=1, keepdims=True)
        scale = lax.rsqrt(square * (1.0 / D) + 1e-05)
        for g in range(KV_HEADS):
            held[g] = ((held[g].astype(F32) - mean) * scale).astype(BF)
        experts = erow_ref[...]
        earlier = (ecol_ref[...] == experts) & (iota((TOK, TOK), 0) < iota((TOK, TOK), 1))
        slot = experts * CAP + jnp.sum(earlier.astype(jnp.int32), axis=0, keepdims=True)
        row = iota((2 * PACK_ROWS, TOK), 0)
        expert, half, r = row // (2 * MAIN), row // MAIN % 2, row % MAIN
        hit = slot == expert * CAP + r
        main_hot = jnp.concatenate(
            [(hit & (half == h)).astype(F32).astype(BF) for h in range(2)], axis=1
        )
        hit = slot == expert * CAP + MAIN + r % 2
        extra_hot = jnp.concatenate(
            [
                (hit & (half == n // FOLD) & (r // 2 == n % FOLD)).astype(F32).astype(BF)
                for n in range(KV_HEADS)
            ],
            axis=1,
        )
        for o in range(FOLD):
            pair = jnp.concatenate([held[o], held[FOLD + o]], axis=0)
            send[:, o * GW : (o + 1) * GW] = dot(main_hot, pair).astype(BF)
        every = jnp.concatenate([held[n] for n in range(KV_HEADS)], axis=0)
        send[:, HALF:] = dot(extra_hot, every).astype(BF)


def attend(place, doc_col, expert_col, expert_row, queries, blocks):
    def whole(shape):
        return pl.BlockSpec(shape, lambda g: (0, 0))

    in_specs = [
        pl.BlockSpec(memory_space=pltpu.SMEM),
        whole((TOK, 1)),
        whole((TOK, 1)),
        whole((1, TOK)),
        pl.BlockSpec((TOK, GW), lambda g: (0, g)),
    ]
    in_specs += [pl.BlockSpec((TOK, HW), lambda g: (0, g))] * WINDOW
    in_specs += [pl.BlockSpec((TOK, HW), lambda g: (0, KV_HEADS + g))] * WINDOW
    in_specs += [pl.BlockSpec((TOK, HW), lambda g: (0, 2 * KV_HEADS))] * WINDOW
    return pl.pallas_call(
        attend_kernel,
        grid=(KV_HEADS,),
        in_specs=in_specs,
        out_specs=[
            pl.BlockSpec((TOK, GW), lambda g: (0, g)),
            whole((2 * PACK_ROWS, HALF + GW)),
        ],
        out_shape=[
            jax.ShapeDtypeStruct((TOK, D), BF),
            jax.ShapeDtypeStruct((2 * PACK_ROWS, HALF + GW), BF),
        ],
        scratch_shapes=[
            pltpu.VMEM((TOK, WINDOW * TOK), F32),
            pltpu.VMEM((WINDOW * TOK, HW), BF),
            pltpu.VMEM((WINDOW * TOK, HW), BF),
            pltpu.VMEM((KV_HEADS, TOK, GW), BF),
            pltpu.VMEM((GROUP * TOK, WINDOW * TOK), F32),
            pltpu.VMEM((GROUP * TOK, WINDOW * TOK), BF),
            pltpu.VMEM((GROUP * TOK, 1), F32),
        ],
        compiler_params=pltpu.CompilerParams(vmem_limit_bytes=VMEM),
        cost_estimate=HINT,
        name="attend",
    )(place, doc_col, expert_col, expert_row, queries, *blocks, *blocks, *blocks)


def gate_kernel(count, *refs):
    packs = refs[: 2 * count]
    w_refs = refs[2 * count : 2 * count + 2 * len(UNITS)]
    hidden, pre, rows = refs[2 * count + 2 * len(UNITS) :]
    step = pl.program_id(0)

    @pl.when(step == 0)
    def _():
        pre[...] = jnp.zeros_like(pre)

    for n in range(8):

        @pl.when(step == n)
        def _(n=n):
            h, o = n // FOLD, n % FOLD
            m = iota((EXPERTS * 2, PACK_ROWS), 0)
            c = iota((EXPERTS * 2, PACK_ROWS), 1)
            pick = (c == (m // 2) * MAIN + 2 * o + m % 2).astype(F32).astype(BF)
            for i in range(count):
                pack = packs[2 * i + h]
                lo = i * BLOCK_ROWS
                rows[lo : lo + PACK_ROWS, :] = pack[:, o * GW : (o + 1) * GW]
                rows[lo + PACK_ROWS : lo + BLOCK_ROWS, :] = dot(pick, pack[:, HALF:]).astype(BF)

    x = rows[...]
    for n, w in enumerate(w_refs):
        at = sum(UNITS[: n % len(UNITS)])
        units = slice(at, at + UNITS[n % len(UNITS)])
        pre[n // len(UNITS), units, :] += dot_t(w[...], x)

    @pl.when(step == 7)
    def _():
        for s in range(2):
            x = pre[s]
            hidden[s] = (x * (1.0 / (1.0 + jnp.exp(-x)))).T.astype(BF)


def gate(packs, weights):
    count = len(packs) // 2
    rows = count * BLOCK_ROWS
    return pl.pallas_call(
        lambda *refs: gate_kernel(count, *refs),
        grid=(8,),
        in_specs=[pl.BlockSpec((PACK_ROWS, HALF + GW), lambda i: (0, 0))] * (2 * count)
        + [pl.BlockSpec((units, GW), lambda i: (0, i)) for units in UNITS * 2],
        out_specs=pl.BlockSpec((2, rows, UNIT), lambda i: (0, 0, 0)),
        out_shape=jax.ShapeDtypeStruct((2, rows, UNIT), BF),
        scratch_shapes=[pltpu.VMEM((2, UNIT, rows), F32), pltpu.VMEM((rows, GW), BF)],
        compiler_params=pltpu.CompilerParams(vmem_limit_bytes=VMEM),
        cost_estimate=HINT,
        name="gate",
    )(*packs, *weights)


def down_kernel(count, part, hidden, kept, other, *refs):
    outs = refs[:count]
    extras = refs[count]
    step = pl.program_id(0)
    row = iota((PACK_ROWS, EXPERTS * 2), 0)
    m = iota((PACK_ROWS, EXPERTS * 2), 1)
    put = (row == (m // 2) * MAIN + 2 * step + m % 2).astype(F32).astype(BF)
    product = (dot(hidden[0], kept[...]) + dot(hidden[1], other[...])).astype(BF)
    lanes = pl.ds(pl.multiple_of(step * part, 128), part)
    for i in range(count):
        lo = i * BLOCK_ROWS
        outs[i][:, lanes] = product[lo : lo + PACK_ROWS]
        folded = dot(put, product[lo + PACK_ROWS : lo + BLOCK_ROWS])

        @pl.when(step == 0)
        def _(i=i, folded=folded):
            extras[i] = folded

        @pl.when(step > 0)
        def _(i=i, folded=folded):
            extras[i] += folded

        @pl.when(step == FOLD - 1)
        def _(i=i):
            outs[i][:, FOLD * part :] = extras[i].astype(BF)


def down(hidden, kept, other):
    rows = hidden.shape[1]
    columns = kept.shape[1]
    part = columns // FOLD
    count = rows // BLOCK_ROWS
    return pl.pallas_call(
        lambda *refs: down_kernel(count, part, *refs),
        grid=(FOLD,),
        in_specs=[pl.BlockSpec((2, rows, UNIT), lambda i: (0, 0, 0))]
        + [pl.BlockSpec((UNIT, part), lambda i: (0, i))] * 2,
        out_specs=[pl.BlockSpec((PACK_ROWS, columns + part), lambda i: (0, 0))] * count,
        out_shape=[jax.ShapeDtypeStruct((PACK_ROWS, columns + part), BF)] * count,
        scratch_shapes=[pltpu.VMEM((count, PACK_ROWS, part), F32)],
        compiler_params=pltpu.CompilerParams(vmem_limit_bytes=VMEM),
        cost_estimate=HINT,
        name="down",
    )(hidden, kept, other)


def combine_kernel(att_ref, *refs):
    backs = refs[: len(PIECES)]
    prob_ref, ecol_ref, erow_ref, out_ref = refs[len(PIECES) :]
    experts = ecol_ref[...]
    earlier = (erow_ref[...] == experts) & (iota((TOK, TOK), 1) < iota((TOK, TOK), 0))
    slot = experts * CAP + jnp.sum(earlier.astype(jnp.int32), axis=1, keepdims=True)
    col = iota((TOK, PACK_ROWS), 1)
    expert, r = col // MAIN, col % MAIN
    main_hot = (slot == expert * CAP + r).astype(F32).astype(BF)
    hit = slot == expert * CAP + MAIN + r % 2
    extra_hot = [(hit & (r // 2 == o)).astype(F32).astype(BF) for o in range(FOLD)]
    prob = prob_ref[...]
    at = 0
    for back, columns in zip(backs, PIECES):
        part = columns // FOLD
        for o in range(FOLD):
            y = dot(main_hot, back[:, o * part : (o + 1) * part])
            y += dot(extra_hot[o], back[:, columns:])
            cols = slice(at + o * part, at + (o + 1) * part)
            out_ref[:, cols] = (att_ref[:, cols].astype(F32) + prob * y).astype(BF)
        at += columns


def combine(attended, backs, prob, expert_col, expert_row):
    return pl.pallas_call(
        combine_kernel,
        out_shape=jax.ShapeDtypeStruct((TOK, D), BF),
        compiler_params=pltpu.CompilerParams(vmem_limit_bytes=VMEM),
        cost_estimate=HINT,
        name="combine",
    )(attended, *backs, prob, expert_col, expert_row)


def shift(x, by):
    return lax.ppermute(x, "z", [(i, (i + by) % 4) for i in range(4)])


def on_device(queries, keys_values, doc_ids, expert_ids, gate_probs, w_gate, w_down):
    z = lax.axis_index("z")
    place = lax.axis_index("xh") * 4 + z
    docs = doc_ids[0]
    own = jnp.concatenate(
        [keys_values[0], jnp.broadcast_to(docs.astype(BF)[None, :], (TOK, TOK))], axis=1
    )
    across = lax.ppermute(own, "xh", [(0, 1)])
    blocks = [own]
    for k in (1, 2, 3):
        blocks.append(shift(jnp.where(z + k >= 4, across, own), k))
    blocks.append(across)

    moves = []
    for xh in range(2):
        for xl in range(2):
            for core in range(2):
                moves.append((xh * 4 + xl * 2 + core, core * 4 + (1 - xl) * 2 + xh))

    def after(x, *earlier):
        return lax.optimization_barrier((x, *earlier))[0]

    def fetch(w):
        return lax.ppermute(w, ("xh", "xl", "core"), moves)

    def swap_cores(w):
        return lax.ppermute(w, "core", [(0, 1), (1, 0)])

    def cut(w, sizes, axis):
        at = 0
        for size in sizes:
            yield lax.slice_in_dim(w, at, at + size, axis=axis)
            at += size

    gate_pieces = list(cut(w_gate[0].T, UNITS, 0))
    down_pieces = list(cut(w_down[0], PIECES, 1))
    gate_1 = fetch(after(gate_pieces[0], across))

    expert_col = (expert_ids[0] + EXPERTS // 2) % EXPERTS
    expert_row = expert_col.reshape(1, TOK)
    heads, gate_1, gate_piece, blocks, down_pieces = lax.optimization_barrier(
        (queries[0], gate_1, gate_pieces[1], blocks, down_pieces)
    )
    gate_2 = fetch(gate_piece)
    other_1 = swap_cores(gate_1)
    attended, send = attend(
        place[None], docs.astype(F32).reshape(TOK, 1), expert_col, expert_row, heads, blocks
    )

    def exchange(x):
        shape = x.shape
        x = x.reshape(EXPERTS, -1, shape[1])
        return lax.all_to_all(x, PLANE, split_axis=0, concat_axis=0, tiled=True)

    def add(*xs):
        total = xs[0].astype(F32)
        for x in xs[1:]:
            total = total + x.astype(F32)
        return total.astype(BF)

    send, gate_2, other_1 = lax.optimization_barrier((send, gate_2, other_1))
    other_2 = swap_cores(gate_2)
    mine, other_2, gate_piece = lax.optimization_barrier((exchange(send), other_2, gate_pieces[2]))
    gate_3 = fetch(gate_piece)
    mine_a = mine[:, :MAIN].reshape(PACK_ROWS, HALF + GW)
    mine_b = mine[:, MAIN:].reshape(PACK_ROWS, HALF + GW)
    left_a, right_a = shift(mine_a, 1), shift(mine_a, -1)
    left_b, right_b = shift(mine_b, 1), shift(mine_b, -1)
    left_a, right_a, left_b, right_b, gate_3, *down_pieces = lax.optimization_barrier(
        (left_a, right_a, left_b, right_b, gate_3, *down_pieces)
    )
    far_a = shift(left_a, 1)
    far_b = shift(right_b, -1)
    other_3 = swap_cores(gate_3)
    kept = fetch(down_pieces[0])
    gate_weights = (gate_1, gate_2, gate_3, other_1, other_2, other_3)
    near = gate((left_a, left_b, right_a, right_b, mine_a, mine_b), gate_weights)
    far = gate((far_a, far_b), gate_weights)
    near, far, kept, *down_pieces = lax.optimization_barrier((near, far, kept, *down_pieces))

    backs = []
    for n in range(len(PIECES)):
        other = swap_cores(kept)
        if n + 1 < len(PIECES):
            following = fetch(after(down_pieces[n + 1], kept))
        (far_part,) = down(far, kept, other)
        left_part, right_part, own_part = down(near, kept, other)
        if n + 1 < len(PIECES):
            following = after(following, far_part, own_part)
        way = 1 if n == 0 else -1
        onward, direct = (right_part, left_part) if way == 1 else (left_part, right_part)
        chain = add(onward, shift(far_part, way))
        total = add(own_part, shift(chain, way), shift(direct, -way))
        backs.append(exchange(total).reshape(total.shape))
        kept = following
    out = combine(attended, backs, gate_probs[0], expert_col, expert_row)
    return out[None]


def solution(mesh):
    split = Mesh(mesh.devices.reshape(2, 4, 2, 4, 2), ("xh", "z", "xl", "y", "core"))
    ctx, exp = ("xh", "z"), ("xl", "y", "core")
    return jax.shard_map(
        on_device,
        mesh=split,
        in_specs=(
            P(exp, ctx, None),
            P(exp, ctx, None),
            P(exp, ctx),
            P(exp, ctx, None),
            P(exp, ctx, None),
            P(exp, None, ctx),
            P(exp, ctx, None),
        ),
        out_specs=P(exp, ctx, None),
        check_vma=False,
    )
```

time: 939 us -> 355 us (0.38)
  blocking collectives: 315 us -> 0 us
  waiting for transfers between devices: 432 us -> 152 us
  Pallas kernels: 0 us -> 87.9 us
  matrix products: 60.5 us -> 0 us
  starting transfers between devices: 13.9 us -> 68.9 us
  local copies, waits for them, and re-layouts: 73.3 us -> 27.2 us
  other arithmetic: 28.9 us -> 12.5 us
  between operations: 13.5 us -> 0.24 us
    all_to_all x1 -> x4, waiting for transfers between devices: 379 us -> 38.5 us  [exchange(): return lax.all_to_all(x, PLANE, split_axis=0, concat_axis=0, tiled=True)]
    all_to_all x1 -> x0, blocking collectives: 297 us -> none  [on_device(): lax.all_to_all(copies, ('ctx', 'exp'), split_axis=0, concat_axis=0, tiled...]
    ppermute x0 -> x31, waiting for transfers between devices: none -> 114 us  [the longest x18 69.8 us: shift(): return lax.ppermute(x, 'z', [(i, (i + by) % 4) for i in range(4)])]
    pallas_call x0 -> x10, Pallas kernels: none -> 87.9 us  [the longest x6 37.7 us: down(): pl.pallas_call(lambda *refs: down_kernel(count, part, *refs), grid=(FOLD,...]
    dot_general x6 -> x0, matrix products: 60.5 us -> none  [the longest x1 18.3 us: on_device(): jnp.dot(hidden, down_local, preferred_element_type=jnp.float32)]
    reshape x3 -> x1, local copies, waits for them, and re-layouts: 56.7 us -> 1.62 us  [on_device(): mine_b = mine[:, MAIN:].reshape(PACK_ROWS, HALF + GW)]
    all_gather x1 -> x0, waiting for transfers between devices: 52.3 us -> none  [on_device(): lax.all_gather(keys_values, 'ctx', axis=1, tiled=True)]
    ppermute x0 -> x31, starting transfers between devices: none -> 39.6 us  [the longest x18 26.3 us: shift(): return lax.ppermute(x, 'z', [(i, (i + by) % 4) for i in range(4)])]
  transfers between devices with their start and end apart: 2 -> 35, of which waited for: 2 -> 20; matrix products, arithmetic and copies ran while one was open for 0% -> 10% of each run, Pallas kernels for 0% -> 24%
where the time goes in v1:
time: 355 us; the launch traced here: 349 us
  waiting for transfers between devices  152 us (43%)
  Pallas kernels  87.9 us (25%)
  starting transfers between devices  68.9 us (19%)
  local copies, waits for them, and re-layouts  27.2 us (8%)
  other arithmetic  12.5 us (4%)
    ppermute x18, waiting for transfers between devices, shift(): return lax.ppermute(x, 'z', [(i, (i + by) % 4) for i in range(4)])  69.8 us
    all_to_all x4, waiting for transfers between devices, exchange(): return lax.all_to_all(x, PLANE, split_axis=0, concat_axis=0, tiled=True)  38.5 us
    pallas_call x6, Pallas kernels, down(): pl.pallas_call(lambda *refs: down_kernel(count, part, *refs), grid=(FOLD,...  37.7 us
    pallas_call x2, Pallas kernels, gate(): pl.pallas_call(lambda *refs: gate_kernel(count, *refs), grid=(8,), in_spe...  30.6 us
    all_to_all x4, starting transfers between devices, exchange(): return lax.all_to_all(x, PLANE, split_axis=0, concat_axis=0, tiled=True)  29.3 us
    ppermute x18, starting transfers between devices, shift(): return lax.ppermute(x, 'z', [(i, (i + by) % 4) for i in range(4)])  26.3 us
    ppermute x6, waiting for transfers between devices, fetch(): return lax.ppermute(w, ('xh', 'xl', 'core'), moves)  22.5 us
    slice x6, local copies, waits for them, and re-layouts, cut(): yield lax.slice_in_dim(w, at, at + size, axis=axis)  21.5 us
  transfers between devices with their start and end apart: 35, of which 20 were waited for; matrix products, arithmetic and copies ran while one was open for 10% of the time, Pallas kernels for 24%

profile of v1, /device:TPU:36, one launch (start us, length us, event | category | flops | bytes accessed | tf_op | source)
XLA Modules:
  0.0 348.8 jit_solution(3586668127523002434)
XLA Ops:
  6.9 12.8 %collective-permute-done.refs_4_.refs_9_.refs_14_ = bf16[128,2176]{1,0:T(8,128)(2,1)S(1)} collective-permute-done((bf16[128,2176]{1,0:T(8,128)(2,1)S(1)}, bf16[128,2176]{1,0:T(8,128)(2,1)S(1)}, u32[]{:S(2)}, u32[]{:S(2)}) %collective-permute-start) | collective-permute-done | bytes 557088 | tf_op jit(solution)/shard_map/ppermute | solution.py:304
  38.8 7.0 %collective-permute-done.2.refs_1_.refs_6_.refs_11_ = bf16[128,2176]{1,0:T(8,128)(2,1)S(1)} collective-permute-done((bf16[128,2176]{1,0:T(8,128)(2,1)S(1)}, bf16[128,2176]{1,0:T(8,128)(2,1)S(1)}, u32[]{:S(2)}, u32[]{:S(2)}) %collective-permute-start.2) | collective-permute-done | bytes 557088 | tf_op jit(solution)/shard_map/ppermute | solution.py:294
  54.9 16.0 %attend.1 = (bf16[128,6144]{1,0:T(8,128)(2,1)}, bf16[256,3840]{1,0:T(8,128)(2,1)}) custom-call(s32[1]{0:T(128)} %bitcast.place_ref, f32[128,1]{1,0:T(8,128)S(1)} %copy.11.doc_ref, s32[128,1]{1,0:T(8,128)S(1)} %add_select_fusion.ecol_ref.refs_4_, s32[1,128]{1,0:T(1,128)S(1)} %and_select_fusion.erow_ref.refs_5_, bf16[128,6144]{1,0:T(8,128)(2,1)} %bitcast.42, ...), custom_call_target="tpu_custom_call" | custom-call | flops 1000000 | bytes 100000 | tf_op jit(solution)/shard_map/attend/pallas_call | solution.py:133
  70.9 9.1 %all-to-all-start = ((bf16[16,16,3840]{2,1,0:T(8,128)(2,1)}), bf16[16,16,3840]{2,1,0:T(8,128)(2,1)}, u32[]{:S(2)}, u32[]{:S(2)}) async-start(bf16[16,16,3840]{2,1,0:T(8,128)(2,1)} %bitcast.41), calls=%async_computation | async-start | bytes 3932160 | tf_op jit(solution)/shard_map/all_to_all | solution.py:349
  80.5 4.6 %slice.37 = bf16[336,6144]{1,0:T(8,128)(2,1)} slice(bf16[672,6144]{1,0:T(8,128)(2,1)} %bitcast.38), slice={[336:672], [0:6144]} | slice | bytes 8257536 | tf_op jit(solution)/shard_map/slice | solution.py:328
  85.1 24.9 %all-to-all-done = bf16[16,16,3840]{2,1,0:T(8,128)(2,1)} async-done(((bf16[16,16,3840]{2,1,0:T(8,128)(2,1)}), bf16[16,16,3840]{2,1,0:T(8,128)(2,1)}, u32[]{:S(2)}, u32[]{:S(2)}) %all-to-all-start) | async-done | bytes 1966112 | tf_op jit(solution)/shard_map/all_to_all | solution.py:349
  120.3 20.5 %collective-permute-done.8.refs_0_ = bf16[128,3840]{1,0:T(8,128)(2,1)S(1)} collective-permute-done((bf16[128,3840]{1,0:T(8,128)(2,1)S(1)}, bf16[128,3840]{1,0:T(8,128)(2,1)S(1)}, u32[]{:S(2)}, u32[]{:S(2)}) %collective-permute-start.8) | collective-permute-done | bytes 983072 | tf_op jit(solution)/shard_map/ppermute | solution.py:294
  142.6 16.3 %collective-permute-done.10.refs_1_ = bf16[128,3840]{1,0:T(8,128)(2,1)S(1)} collective-permute-done((bf16[128,3840]{1,0:T(8,128)(2,1)S(1)}, bf16[128,3840]{1,0:T(8,128)(2,1)S(1)}, u32[]{:S(2)}, u32[]{:S(2)}) %collective-permute-start.10) | collective-permute-done | bytes 983072 | tf_op jit(solution)/shard_map/ppermute | solution.py:294
  167.8 19.3 %gate.2.refs_0_ = bf16[2,480,672]{2,1,0:T(8,128)(2,1)} custom-call(bf16[128,3840]{1,0:T(8,128)(2,1)S(1)} %collective-permute-done.8.refs_0_, bf16[128,3840]{1,0:T(8,128)(2,1)S(1)} %collective-permute-done.10.refs_1_, bf16[128,3840]{1,0:T(8,128)(2,1)S(1)} %collective-permute-done.9.refs_2_, bf16[128,3840]{1,0:T(8,128)(2,1)S(1)} %collective-permute-done.11.refs_3_, ...), custom_call_target="tpu_custom_call" | custom-call | flops 1000000 | bytes 100000 | tf_op jit(solution)/shard_map/gate/pallas_call | solution.py:200
  187.1 11.4 %gate.3.refs_0_ = bf16[2,160,672]{2,1,0:T(8,128)(2,1)S(1)} custom-call(bf16[128,3840]{1,0:T(8,128)(2,1)S(1)} %collective-permute-done.14.refs_0_, bf16[128,3840]{1,0:T(8,128)(2,1)S(1)} %collective-permute-done.15.refs_1_, bf16[224,6144]{1,0:T(8,128)(2,1)} %collective-permute-done.1.refs_6_.refs_2_, bf16[112,6144]{1,0:T(8,128)(2,1)S(1)} %copy-done.3, ...), custom_call_target="tpu_custom_call" | custom-call | flops 1000000 | bytes 100000 | tf_op jit(solution)/shard_map/gate/pallas_call | solution.py:200
  198.5 10.2 %collective-permute-done.16.refs_1_ = bf16[672,3072]{1,0:T(8,128)(2,1)S(1)} collective-permute-done((bf16[672,3072]{1,0:T(8,128)(2,1)}, bf16[672,3072]{1,0:T(8,128)(2,1)S(1)}, u32[]{:S(2)}, u32[]{:S(2)}) %collective-permute-start.16) | collective-permute-done | bytes 4128800 | tf_op jit(solution)/shard_map/ppermute | solution.py:320
  211.0 4.9 %collective-permute-done.17.refs_2_ = bf16[672,3072]{1,0:T(8,128)(2,1)} collective-permute-done((bf16[672,3072]{1,0:T(8,128)(2,1)S(1)}, bf16[672,3072]{1,0:T(8,128)(2,1)}, u32[]{:S(2)}, u32[]{:S(2)}) %collective-permute-start.17) | collective-permute-done | bytes 4128800 | tf_op jit(solution)/shard_map/ppermute | solution.py:323
  215.9 10.4 %down.6 = (bf16[128,3840]{1,0:T(8,128)(2,1)S(1)}, bf16[128,3840]{1,0:T(8,128)(2,1)S(1)}, bf16[128,3840]{1,0:T(8,128)(2,1)S(1)}) custom-call(bf16[2,480,672]{2,1,0:T(8,128)(2,1)} %gate.2.refs_0_, bf16[672,3072]{1,0:T(8,128)(2,1)} %copy-done.12, bf16[672,3072]{1,0:T(8,128)(2,1)} %collective-permute-done.17.refs_2_), custom_call_target="tpu_custom_call" | custom-call | flops 1000000 | bytes 100000 | tf_op jit(solution)/shard_map/down/pallas_call | solution.py:246
  226.4 5.7 %down.7 = bf16[128,3840]{1,0:T(8,128)(2,1)S(1)} custom-call(bf16[2,160,672]{2,1,0:T(8,128)(2,1)S(1)} %gate.3.refs_0_, bf16[672,3072]{1,0:T(8,128)(2,1)} %copy-done.12, bf16[672,3072]{1,0:T(8,128)(2,1)} %collective-permute-done.17.refs_2_), custom_call_target="tpu_custom_call" | custom-call | flops 1000000 | bytes 100000 | tf_op jit(solution)/shard_map/down/pallas_call | solution.py:246
  232.1 9.9 %collective-permute-done.21.refs_1_ = bf16[672,2048]{1,0:T(8,128)(2,1)S(1)} collective-permute-done((bf16[672,2048]{1,0:T(8,128)(2,1)}, bf16[672,2048]{1,0:T(8,128)(2,1)S(1)}, u32[]{:S(2)}, u32[]{:S(2)}) %collective-permute-start.21) | collective-permute-done | bytes 2752544 | tf_op jit(solution)/shard_map/ppermute | solution.py:320
  252.9 7.9 %down.8 = (bf16[128,2560]{1,0:T(8,128)(2,1)S(1)}, bf16[128,2560]{1,0:T(8,128)(2,1)}, bf16[128,2560]{1,0:T(8,128)(2,1)S(1)}) custom-call(bf16[2,480,672]{2,1,0:T(8,128)(2,1)S(1)} %copy-done, bf16[672,2048]{1,0:T(8,128)(2,1)} %copy-done.1, bf16[672,2048]{1,0:T(8,128)(2,1)} %collective-permute-done.22.refs_2_), custom_call_target="tpu_custom_call" | custom-call | flops 1000000 | bytes 100000 | tf_op jit(solution)/shard_map/down/pallas_call | solution.py:246
  260.8 7.3 %collective-permute-done.18 = bf16[128,3840]{1,0:T(8,128)(2,1)S(1)} collective-permute-done((bf16[128,3840]{1,0:T(8,128)(2,1)S(1)}, bf16[128,3840]{1,0:T(8,128)(2,1)S(1)}, u32[]{:S(2)}, u32[]{:S(2)}) %collective-permute-start.18) | collective-permute-done | bytes 983072 | tf_op jit(solution)/shard_map/ppermute | solution.py:294
  271.9 12.0 %collective-permute-done.23 = bf16[128,2560]{1,0:T(8,128)(2,1)} collective-permute-done((bf16[128,2560]{1,0:T(8,128)(2,1)S(1)}, bf16[128,2560]{1,0:T(8,128)(2,1)}, u32[]{:S(2)}, u32[]{:S(2)}) %collective-permute-start.23) | collective-permute-done | bytes 655392 | tf_op jit(solution)/shard_map/ppermute | solution.py:294
  296.0 7.6 %all-to-all-start.1 = ((bf16[16,8,3840]{2,1,0:T(8,128)(2,1)}), bf16[16,8,3840]{2,1,0:T(8,128)(2,1)}, u32[]{:S(2)}, u32[]{:S(2)}) async-start(bf16[16,8,3840]{2,1,0:T(8,128)(2,1)} %fusion), calls=%async_computation.1 | async-start | bytes 1966080 | tf_op jit(solution)/shard_map/all_to_all | solution.py:349
  303.6 6.4 %down.10 = (bf16[128,1280]{1,0:T(8,128)(2,1)S(1)}, bf16[128,1280]{1,0:T(8,128)(2,1)}, bf16[128,1280]{1,0:T(8,128)(2,1)S(1)}) custom-call(bf16[2,480,672]{2,1,0:T(8,128)(2,1)} %gate.2.refs_0_, bf16[672,1024]{1,0:T(8,128)(2,1)S(1)} %collective-permute-done.26.refs_1_, bf16[672,1024]{1,0:T(8,128)(2,1)S(1)} %collective-permute-done.27.refs_2_), custom_call_target="tpu_custom_call" | custom-call | flops 1000000 | bytes 100000 | tf_op jit(solution)/shard_map/down/pallas_call | solution.py:246
  317.3 7.1 %all-to-all-start.2 = ((bf16[16,8,2560]{2,1,0:T(8,128)(2,1)}), bf16[16,8,2560]{2,1,0:T(8,128)(2,1)S(1)}, u32[]{:S(2)}, u32[]{:S(2)}) async-start(bf16[16,8,2560]{2,1,0:T(8,128)(2,1)} %fusion.1), calls=%async_computation.2 | async-start | bytes 1310720 | tf_op jit(solution)/shard_map/all_to_all | solution.py:349
  326.3 6.7 %all-to-all-done.2 = bf16[16,8,2560]{2,1,0:T(8,128)(2,1)S(1)} async-done(((bf16[16,8,2560]{2,1,0:T(8,128)(2,1)}), bf16[16,8,2560]{2,1,0:T(8,128)(2,1)S(1)}, u32[]{:S(2)}, u32[]{:S(2)}) %all-to-all-start.2) | async-done | bytes 655392 | tf_op jit(solution)/shard_map/all_to_all | solution.py:349
  332.9 5.5 %all-to-all-start.3 = ((bf16[16,8,1280]{2,1,0:T(8,128)(2,1)}), bf16[16,8,1280]{2,1,0:T(8,128)(2,1)S(1)}, u32[]{:S(2)}, u32[]{:S(2)}) async-start(bf16[16,8,1280]{2,1,0:T(8,128)(2,1)} %fusion.2), calls=%async_computation.3 | async-start | bytes 655360 | tf_op jit(solution)/shard_map/all_to_all | solution.py:349
  338.6 6.7 %all-to-all-done.3 = bf16[16,8,1280]{2,1,0:T(8,128)(2,1)S(1)} async-done(((bf16[16,8,1280]{2,1,0:T(8,128)(2,1)}), bf16[16,8,1280]{2,1,0:T(8,128)(2,1)S(1)}, u32[]{:S(2)}, u32[]{:S(2)}) %all-to-all-start.3) | async-done | bytes 327712 | tf_op jit(solution)/shard_map/all_to_all | solution.py:349
  (119 shorter events, 98.6 us)
Async XLA Ops:
  19.6 32.8 %collective-permute-start.1 = (bf16[224,6144]{1,0:T(8,128)(2,1)}, bf16[224,6144]{1,0:T(8,128)(2,1)}, u32[]{:S(2)}, u32[]{:S(2)}) collective-permute-start(bf16[224,6144]{1,0:T(8,128)(2,1)} %slice.32), channel_id=1, source_target_pairs={{0,8},{1,72},{8,0},{9,64},{64,9},{65,73},{72,1},{73,65},{2,10},{3,... | collective-permute-start | bytes 8257544 | tf_op jit(solution)/shard_map/ppermute | solution.py:320
  19.9 25.9 %collective-permute-start.2 = (bf16[128,2176]{1,0:T(8,128)(2,1)S(1)}, bf16[128,2176]{1,0:T(8,128)(2,1)S(1)}, u32[]{:S(2)}, u32[]{:S(2)}) collective-permute-start(bf16[128,2176]{1,0:T(8,128)(2,1)S(1)} %get-tuple-element.101), channel_id=1, source_target_pairs={{0,16},{16,32},{32,48},{48,0},{1,17},{17,33},{33,49},{49,1},{2,18}... | collective-permute-start | bytes 1671176 | tf_op jit(solution)/shard_map/ppermute | solution.py:294
  21.9 23.9 %collective-permute-start.3 = (bf16[128,2176]{1,0:T(8,128)(2,1)S(1)}, bf16[128,2176]{1,0:T(8,128)(2,1)S(1)}, u32[]{:S(2)}, u32[]{:S(2)}) collective-permute-start(bf16[128,2176]{1,0:T(8,128)(2,1)S(1)} %get-tuple-element.100), channel_id=1, source_target_pairs={{0,32},{16,48},{32,0},{48,16},{1,33},{17,49},{33,1},{49,17},{2,34}... | collective-permute-start | bytes 1671176 | tf_op jit(solution)/shard_map/ppermute | solution.py:294
  23.1 26.1 %collective-permute-start.4 = (bf16[128,2176]{1,0:T(8,128)(2,1)S(1)}, bf16[128,2176]{1,0:T(8,128)(2,1)S(1)}, u32[]{:S(2)}, u32[]{:S(2)}) collective-permute-start(bf16[128,2176]{1,0:T(8,128)(2,1)S(1)} %get-tuple-element.99), channel_id=1, source_target_pairs={{0,48},{16,0},{32,16},{48,32},{1,49},{17,1},{33,17},{49,33},{2,50}... | collective-permute-start | bytes 1671176 | tf_op jit(solution)/shard_map/ppermute | solution.py:294
  70.9 39.1 %all-to-all-start = ((bf16[16,16,3840]{2,1,0:T(8,128)(2,1)}), bf16[16,16,3840]{2,1,0:T(8,128)(2,1)}, u32[]{:S(2)}, u32[]{:S(2)}) async-start(bf16[16,16,3840]{2,1,0:T(8,128)(2,1)} %bitcast.41), calls=%async_computation | async-start | bytes 3932160 | tf_op jit(solution)/shard_map/all_to_all | solution.py:349
  110.0 50.6 %collective-permute-start.12 = (bf16[336,6144]{1,0:T(8,128)(2,1)}, bf16[336,6144]{1,0:T(8,128)(2,1)S(1)}, u32[]{:S(2)}, u32[]{:S(2)}) collective-permute-start(bf16[336,6144]{1,0:T(8,128)(2,1)} %slice.37), channel_id=1, source_target_pairs={{0,8},{1,72},{8,0},{9,64},{64,9},{65,73},{72,1},{73,65},{2,10},{3,... | collective-permute-start | bytes 12386312 | tf_op jit(solution)/shard_map/ppermute | solution.py:320
  116.0 24.8 %collective-permute-start.8 = (bf16[128,3840]{1,0:T(8,128)(2,1)S(1)}, bf16[128,3840]{1,0:T(8,128)(2,1)S(1)}, u32[]{:S(2)}, u32[]{:S(2)}) collective-permute-start(bf16[128,3840]{1,0:T(8,128)(2,1)S(1)} %get-tuple-element.98.refs_4_), channel_id=1, source_target_pairs={{0,16},{16,32},{32,48},{48,0},{1,17},{17,33},{33,49},{49,1},{2,18}... | collective-permute-start | bytes 2949128 | tf_op jit(solution)/shard_map/ppermute | solution.py:294
  118.0 24.7 %collective-permute-start.9 = (bf16[128,3840]{1,0:T(8,128)(2,1)S(1)}, bf16[128,3840]{1,0:T(8,128)(2,1)S(1)}, u32[]{:S(2)}, u32[]{:S(2)}) collective-permute-start(bf16[128,3840]{1,0:T(8,128)(2,1)S(1)} %get-tuple-element.98.refs_4_), channel_id=1, source_target_pairs={{0,48},{16,0},{32,16},{48,32},{1,49},{17,1},{33,17},{49,33},{2,50}... | collective-permute-start | bytes 2949128 | tf_op jit(solution)/shard_map/ppermute | solution.py:294
  118.1 40.9 %collective-permute-start.10 = (bf16[128,3840]{1,0:T(8,128)(2,1)S(1)}, bf16[128,3840]{1,0:T(8,128)(2,1)S(1)}, u32[]{:S(2)}, u32[]{:S(2)}) collective-permute-start(bf16[128,3840]{1,0:T(8,128)(2,1)S(1)} %get-tuple-element.97.refs_5_), channel_id=1, source_target_pairs={{0,16},{16,32},{32,48},{48,0},{1,17},{17,33},{33,49},{49,1},{2,18}... | collective-permute-start | bytes 2949128 | tf_op jit(solution)/shard_map/ppermute | solution.py:294
  120.0 40.6 %collective-permute-start.11 = (bf16[128,3840]{1,0:T(8,128)(2,1)S(1)}, bf16[128,3840]{1,0:T(8,128)(2,1)S(1)}, u32[]{:S(2)}, u32[]{:S(2)}) collective-permute-start(bf16[128,3840]{1,0:T(8,128)(2,1)S(1)} %get-tuple-element.97.refs_5_), channel_id=1, source_target_pairs={{0,48},{16,0},{32,16},{48,32},{1,49},{17,1},{33,17},{49,33},{2,50}... | collective-permute-start | bytes 2949128 | tf_op jit(solution)/shard_map/ppermute | solution.py:294
  160.6 48.1 %collective-permute-start.16 = (bf16[672,3072]{1,0:T(8,128)(2,1)}, bf16[672,3072]{1,0:T(8,128)(2,1)S(1)}, u32[]{:S(2)}, u32[]{:S(2)}) collective-permute-start(bf16[672,3072]{1,0:T(8,128)(2,1)} %slice.34), channel_id=1, source_target_pairs={{0,8},{1,72},{8,0},{9,64},{64,9},{65,73},{72,1},{73,65},{2,10},{3,... | collective-permute-start | bytes 12386312 | tf_op jit(solution)/shard_map/ppermute | solution.py:320
  163.0 24.1 %collective-permute-start.14 = (bf16[128,3840]{1,0:T(8,128)(2,1)S(1)}, bf16[128,3840]{1,0:T(8,128)(2,1)S(1)}, u32[]{:S(2)}, u32[]{:S(2)}) collective-permute-start(bf16[128,3840]{1,0:T(8,128)(2,1)S(1)} %collective-permute-done.8.refs_0_), channel_id=1, source_target_pairs={{0,16},{16,32},{32,48},{48,0},{1,17},{17,33},{33,49},{49,1},{2,18}... | collective-permute-start | bytes 2949128 | tf_op jit(solution)/shard_map/ppermute | solution.py:294
  164.9 22.2 %collective-permute-start.15 = (bf16[128,3840]{1,0:T(8,128)(2,1)S(1)}, bf16[128,3840]{1,0:T(8,128)(2,1)S(1)}, u32[]{:S(2)}, u32[]{:S(2)}) collective-permute-start(bf16[128,3840]{1,0:T(8,128)(2,1)S(1)} %collective-permute-done.11.refs_3_), channel_id=1, source_target_pairs={{0,48},{16,0},{32,16},{48,32},{1,49},{17,1},{33,17},{49,33},{2,50}... | collective-permute-start | bytes 2949128 | tf_op jit(solution)/shard_map/ppermute | solution.py:294
  208.7 33.3 %collective-permute-start.21 = (bf16[672,2048]{1,0:T(8,128)(2,1)}, bf16[672,2048]{1,0:T(8,128)(2,1)S(1)}, u32[]{:S(2)}, u32[]{:S(2)}) collective-permute-start(bf16[672,2048]{1,0:T(8,128)(2,1)} %slice.35), channel_id=1, source_target_pairs={{0,8},{1,72},{8,0},{9,64},{64,9},{65,73},{72,1},{73,65},{2,10},{3,... | collective-permute-start | bytes 8257544 | tf_op jit(solution)/shard_map/ppermute | solution.py:320
  242.0 18.8 %collective-permute-start.26 = (bf16[672,1024]{1,0:T(8,128)(2,1)S(1)}, bf16[672,1024]{1,0:T(8,128)(2,1)S(1)}, u32[]{:S(2)}, u32[]{:S(2)}) collective-permute-start(bf16[672,1024]{1,0:T(8,128)(2,1)S(1)} %copy-done.17), channel_id=1, source_target_pairs={{0,8},{1,72},{8,0},{9,64},{64,9},{65,73},{72,1},{73,65},{2,10},{3,... | collective-permute-start | bytes 4128776 | tf_op jit(solution)/shard_map/ppermute | solution.py:320
  244.4 23.7 %collective-permute-start.18 = (bf16[128,3840]{1,0:T(8,128)(2,1)S(1)}, bf16[128,3840]{1,0:T(8,128)(2,1)S(1)}, u32[]{:S(2)}, u32[]{:S(2)}) collective-permute-start(bf16[128,3840]{1,0:T(8,128)(2,1)S(1)} %down.7), channel_id=1, source_target_pairs={{0,16},{16,32},{32,48},{48,0},{1,17},{17,33},{33,49},{49,1},{2,18}... | collective-permute-start | bytes 2949128 | tf_op jit(solution)/shard_map/ppermute | solution.py:294
  246.3 46.4 %collective-permute-start.20 = (bf16[128,3840]{1,0:T(8,128)(2,1)S(1)}, bf16[128,3840]{1,0:T(8,128)(2,1)}, u32[]{:S(2)}, u32[]{:S(2)}) collective-permute-start(bf16[128,3840]{1,0:T(8,128)(2,1)S(1)} %get-tuple-element.84), channel_id=1, source_target_pairs={{0,48},{16,0},{32,16},{48,32},{1,49},{17,1},{33,17},{49,33},{2,50}... | collective-permute-start | bytes 2949128 | tf_op jit(solution)/shard_map/ppermute | solution.py:294
  251.5 32.4 %collective-permute-start.23 = (bf16[128,2560]{1,0:T(8,128)(2,1)S(1)}, bf16[128,2560]{1,0:T(8,128)(2,1)}, u32[]{:S(2)}, u32[]{:S(2)}) collective-permute-start(bf16[128,2560]{1,0:T(8,128)(2,1)S(1)} %down.9), channel_id=1, source_target_pairs={{0,48},{16,0},{32,16},{48,32},{1,49},{17,1},{33,17},{49,33},{2,50}... | collective-permute-start | bytes 1966088 | tf_op jit(solution)/shard_map/ppermute | solution.py:294
  260.8 25.5 %collective-permute-start.27 = (bf16[672,1024]{1,0:T(8,128)(2,1)S(1)}, bf16[672,1024]{1,0:T(8,128)(2,1)S(1)}, u32[]{:S(2)}, u32[]{:S(2)}) collective-permute-start(bf16[672,1024]{1,0:T(8,128)(2,1)S(1)} %collective-permute-done.26.refs_1_), channel_id=1, source_target_pairs={{0,1},{1,0},{2,3},{3,2},{4,5},{5,4},{6,7},{7,6},{8,9},{9,8},{10,11... | collective-permute-start | bytes 4128776 | tf_op jit(solution)/shard_map/ppermute | solution.py:323
  268.3 25.1 %collective-permute-start.19 = (bf16[128,3840]{1,0:T(8,128)(2,1)S(1)}, bf16[128,3840]{1,0:T(8,128)(2,1)S(1)}, u32[]{:S(2)}, u32[]{:S(2)}) collective-permute-start(bf16[128,3840]{1,0:T(8,128)(2,1)S(1)} %add_convert_fusion.1), channel_id=1, source_target_pairs={{0,16},{16,32},{32,48},{48,0},{1,17},{17,33},{33,49},{49,1},{2,18}... | collective-permute-start | bytes 2949128 | tf_op jit(solution)/shard_map/ppermute | solution.py:294
  270.3 44.3 %collective-permute-start.25 = (bf16[128,2560]{1,0:T(8,128)(2,1)}, bf16[128,2560]{1,0:T(8,128)(2,1)}, u32[]{:S(2)}, u32[]{:S(2)}) collective-permute-start(bf16[128,2560]{1,0:T(8,128)(2,1)} %get-tuple-element.90), channel_id=1, source_target_pairs={{0,16},{16,32},{32,48},{48,0},{1,17},{17,33},{33,49},{49,1},{2,18}... | collective-permute-start | bytes 1966088 | tf_op jit(solution)/shard_map/ppermute | solution.py:294
  286.0 28.6 %collective-permute-start.24 = (bf16[128,2560]{1,0:T(8,128)(2,1)}, bf16[128,2560]{1,0:T(8,128)(2,1)}, u32[]{:S(2)}, u32[]{:S(2)}) collective-permute-start(bf16[128,2560]{1,0:T(8,128)(2,1)} %add_convert_fusion.3), channel_id=1, source_target_pairs={{0,48},{16,0},{32,16},{48,32},{1,49},{17,1},{33,17},{49,33},{2,50}... | collective-permute-start | bytes 1966088 | tf_op jit(solution)/shard_map/ppermute | solution.py:294
  289.3 22.4 %collective-permute-start.28 = (bf16[128,1280]{1,0:T(8,128)(2,1)}, bf16[128,1280]{1,0:T(8,128)(2,1)}, u32[]{:S(2)}, u32[]{:S(2)}) collective-permute-start(bf16[128,1280]{1,0:T(8,128)(2,1)} %down.11), channel_id=1, source_target_pairs={{0,48},{16,0},{32,16},{48,32},{1,49},{17,1},{33,17},{49,33},{2,50}... | collective-permute-start | bytes 983048 | tf_op jit(solution)/shard_map/ppermute | solution.py:294
  296.0 21.4 %all-to-all-start.1 = ((bf16[16,8,3840]{2,1,0:T(8,128)(2,1)}), bf16[16,8,3840]{2,1,0:T(8,128)(2,1)}, u32[]{:S(2)}, u32[]{:S(2)}) async-start(bf16[16,8,3840]{2,1,0:T(8,128)(2,1)} %fusion), calls=%async_computation.1 | async-start | bytes 1966080 | tf_op jit(solution)/shard_map/all_to_all | solution.py:349
  (31 other events, 493.6 us)

commit v2 on v1

--- a/solution.py
+++ b/solution.py
@@ -22,13 +22,16 @@
 UNIT = 672
 PACK_ROWS = EXPERTS * MAIN
 BLOCK_ROWS = EXPERTS * CAP
-PIECES = (3072, 2048, 1024)
-UNITS = (224, 112, 336)
+PIECES = (1536, 2560, 2048)
+UNITS = (208, 128, 336)
 VMEM = 50 * 1024 * 1024
 PLANE = ("xl", "y", "xh")
-HINT = pl.CostEstimate(flops=10**6, bytes_accessed=10**5, transcendentals=0)
 BF = jnp.bfloat16
 F32 = jnp.float32
+
+
+def cost(microseconds):
+    return pl.CostEstimate(flops=10**9 * microseconds, bytes_accessed=10**6, transcendentals=0)
 
 
 def iota(shape, axis):
@@ -152,7 +155,7 @@
             pltpu.VMEM((GROUP * TOK, 1), F32),
         ],
         compiler_params=pltpu.CompilerParams(vmem_limit_bytes=VMEM),
-        cost_estimate=HINT,
+        cost_estimate=cost(16),
         name="attend",
     )(place, doc_col, expert_col, expert_row, queries, *blocks, *blocks, *blocks)
 
@@ -197,28 +200,36 @@
 def gate(packs, weights):
     count = len(packs) // 2
     rows = count * BLOCK_ROWS
+    pack_specs = [pl.BlockSpec((PACK_ROWS, HALF + GW), lambda i, at=at: (at, 0)) for _, at in packs]
     return pl.pallas_call(
         lambda *refs: gate_kernel(count, *refs),
         grid=(8,),
-        in_specs=[pl.BlockSpec((PACK_ROWS, HALF + GW), lambda i: (0, 0))] * (2 * count)
+        in_specs=pack_specs
         + [pl.BlockSpec((units, GW), lambda i: (0, i)) for units in UNITS * 2],
         out_specs=pl.BlockSpec((2, rows, UNIT), lambda i: (0, 0, 0)),
         out_shape=jax.ShapeDtypeStruct((2, rows, UNIT), BF),
         scratch_shapes=[pltpu.VMEM((2, UNIT, rows), F32), pltpu.VMEM((rows, GW), BF)],
         compiler_params=pltpu.CompilerParams(vmem_limit_bytes=VMEM),
-        cost_estimate=HINT,
+        cost_estimate=cost(8 + rows // 40),
         name="gate",
-    )(*packs, *weights)
-
-
-def down_kernel(count, part, hidden, kept, other, *refs):
-    outs = refs[:count]
-    extras = refs[count]
+    )(*[pack for pack, _ in packs], *weights)
+
+
+def down_kernel(count, part, fetches, hidden, *refs):
+    w_refs = refs[: 2 * fetches]
+    outs = refs[2 * fetches : 2 * fetches + count]
+    extras = refs[2 * fetches + count]
     step = pl.program_id(0)
     row = iota((PACK_ROWS, EXPERTS * 2), 0)
     m = iota((PACK_ROWS, EXPERTS * 2), 1)
     put = (row == (m // 2) * MAIN + 2 * step + m % 2).astype(F32).astype(BF)
-    product = (dot(hidden[0], kept[...]) + dot(hidden[1], other[...])).astype(BF)
+    if fetches == 1:
+        kept, other = (w[...] for w in w_refs)
+    else:
+        late = step >= FOLD // 2
+        kept = jnp.where(late, w_refs[1][...], w_refs[0][...])
+        other = jnp.where(late, w_refs[3][...], w_refs[2][...])
+    product = (dot(hidden[0], kept) + dot(hidden[1], other)).astype(BF)
     lanes = pl.ds(pl.multiple_of(step * part, 128), part)
     for i in range(count):
         lo = i * BLOCK_ROWS
@@ -238,28 +249,37 @@
             outs[i][:, FOLD * part :] = extras[i].astype(BF)
 
 
-def down(hidden, kept, other):
+def down(hidden, kept, other, microseconds=0):
+    kept, other = (kept,), (other,)
     rows = hidden.shape[1]
-    columns = kept.shape[1]
+    fetches = len(kept)
+    columns = sum(w.shape[1] for w in kept)
     part = columns // FOLD
     count = rows // BLOCK_ROWS
+    if fetches == 1:
+        w_specs = [pl.BlockSpec((UNIT, part), lambda i: (0, i))]
+    else:
+        w_specs = [
+            pl.BlockSpec((UNIT, part), lambda i: (0, jnp.minimum(i, 1))),
+            pl.BlockSpec((UNIT, part), lambda i: (0, jnp.maximum(i - 2, 0))),
+        ]
     return pl.pallas_call(
-        lambda *refs: down_kernel(count, part, *refs),
+        lambda *refs: down_kernel(count, part, fetches, *refs),
         grid=(FOLD,),
-        in_specs=[pl.BlockSpec((2, rows, UNIT), lambda i: (0, 0, 0))]
-        + [pl.BlockSpec((UNIT, part), lambda i: (0, i))] * 2,
+        in_specs=[pl.BlockSpec((2, rows, UNIT), lambda i: (0, 0, 0))] + w_specs * 2,
         out_specs=[pl.BlockSpec((PACK_ROWS, columns + part), lambda i: (0, 0))] * count,
         out_shape=[jax.ShapeDtypeStruct((PACK_ROWS, columns + part), BF)] * count,
         scratch_shapes=[pltpu.VMEM((count, PACK_ROWS, part), F32)],
         compiler_params=pltpu.CompilerParams(vmem_limit_bytes=VMEM),
-        cost_estimate=HINT,
+        cost_estimate=cost(microseconds),
         name="down",
-    )(hidden, kept, other)
+    )(hidden, *kept, *other)
 
 
 def combine_kernel(att_ref, *refs):
-    backs = refs[: len(PIECES)]
-    prob_ref, ecol_ref, erow_ref, out_ref = refs[len(PIECES) :]
+    first, second, prob_ref, ecol_ref, erow_ref, out_ref = refs
+    split = PIECES[1] + PIECES[1] // FOLD
+    backs = (first, second.at[:, :split], second.at[:, split:])
     experts = ecol_ref[...]
     earlier = (erow_ref[...] == experts) & (iota((TOK, TOK), 1) < iota((TOK, TOK), 0))
     slot = experts * CAP + jnp.sum(earlier.astype(jnp.int32), axis=1, keepdims=True)
@@ -285,7 +305,7 @@
         combine_kernel,
         out_shape=jax.ShapeDtypeStruct((TOK, D), BF),
         compiler_params=pltpu.CompilerParams(vmem_limit_bytes=VMEM),
-        cost_estimate=HINT,
+        cost_estimate=cost(3),
         name="combine",
     )(attended, *backs, prob, expert_col, expert_row)
 
@@ -313,6 +333,8 @@
             for core in range(2):
                 moves.append((xh * 4 + xl * 2 + core, core * 4 + (1 - xl) * 2 + xh))
 
+    barrier = lax.optimization_barrier
+
     def after(x, *earlier):
         return lax.optimization_barrier((x, *earlier))[0]
 
@@ -356,39 +378,57 @@
 
     send, gate_2, other_1 = lax.optimization_barrier((send, gate_2, other_1))
     other_2 = swap_cores(gate_2)
-    mine, other_2, gate_piece = lax.optimization_barrier((exchange(send), other_2, gate_pieces[2]))
+    back, other_2, gate_piece = lax.optimization_barrier((exchange(send), other_2, gate_pieces[2]))
+    mine = back.reshape(EXPERTS, 2, MAIN, HALF + GW).transpose(1, 0, 2, 3)
+    mine = mine.reshape(2 * PACK_ROWS, HALF + GW)
     gate_3 = fetch(gate_piece)
-    mine_a = mine[:, :MAIN].reshape(PACK_ROWS, HALF + GW)
-    mine_b = mine[:, MAIN:].reshape(PACK_ROWS, HALF + GW)
-    left_a, right_a = shift(mine_a, 1), shift(mine_a, -1)
-    left_b, right_b = shift(mine_b, 1), shift(mine_b, -1)
-    left_a, right_a, left_b, right_b, gate_3, *down_pieces = lax.optimization_barrier(
-        (left_a, right_a, left_b, right_b, gate_3, *down_pieces)
-    )
-    far_a = shift(left_a, 1)
-    far_b = shift(right_b, -1)
+    left, right, gate_3, down_pieces = lax.optimization_barrier(
+        (shift(mine, 1), shift(mine, -1), gate_3, down_pieces)
+    )
+    far_a = shift(left[:PACK_ROWS], 1)
+    far_b = shift(right[PACK_ROWS:], -1)
     other_3 = swap_cores(gate_3)
-    kept = fetch(down_pieces[0])
+    kept_a = fetch(down_pieces[0])
     gate_weights = (gate_1, gate_2, gate_3, other_1, other_2, other_3)
-    near = gate((left_a, left_b, right_a, right_b, mine_a, mine_b), gate_weights)
-    far = gate((far_a, far_b), gate_weights)
-    near, far, kept, *down_pieces = lax.optimization_barrier((near, far, kept, *down_pieces))
-
-    backs = []
-    for n in range(len(PIECES)):
-        other = swap_cores(kept)
-        if n + 1 < len(PIECES):
-            following = fetch(after(down_pieces[n + 1], kept))
-        (far_part,) = down(far, kept, other)
-        left_part, right_part, own_part = down(near, kept, other)
-        if n + 1 < len(PIECES):
-            following = after(following, far_part, own_part)
-        way = 1 if n == 0 else -1
-        onward, direct = (right_part, left_part) if way == 1 else (left_part, right_part)
-        chain = add(onward, shift(far_part, way))
-        total = add(own_part, shift(chain, way), shift(direct, -way))
-        backs.append(exchange(total).reshape(total.shape))
-        kept = following
+    near = gate([(x, at) for x in (left, right, mine) for at in range(2)], gate_weights)
+    near, far_a, far_b, kept_a, down_pieces = barrier((near, far_a, far_b, kept_a, down_pieces))
+    far = gate([(far_a, 0), (far_b, 0)], gate_weights)
+    kept_b = fetch(down_pieces[1])
+    other_a = swap_cores(kept_a)
+    far, other_a, down_pieces = barrier((far, other_a, down_pieces))
+
+    (far_part,) = down(far, kept_a, other_a, 4)
+    left_part, right_part, own_a = down(after(near, far_part), kept_a, other_a, 8)
+    passed, direct_a, right_part, kept_b = barrier(
+        (shift(far_part, 1), shift(left_part, -1), right_part, kept_b)
+    )
+    kept_c = fetch(after(down_pieces[2], kept_b))
+    other_b = swap_cores(kept_b)
+    chain_a = add(right_part, passed)
+    (far_part,) = down(far, kept_b, other_b, 4)
+    left_part, right_part, own_b = down(after(near, far_part), kept_b, other_b, 8)
+    summed_a, passed, left_part, right_part, kept_c = barrier(
+        (shift(chain_a, 1), shift(far_part, -1), left_part, right_part, kept_c)
+    )
+    other_c = swap_cores(kept_c)
+    back_a = exchange(add(own_a, summed_a, direct_a))
+    chain_b = add(left_part, passed)
+    (far_c,) = down(far, kept_c, other_c, 3)
+    left_c, right_c, own_c = down(after(near, far_c), kept_c, other_c, 6)
+    summed_b, direct_b, far_c, left_c, right_c, back_a = barrier(
+        (
+            shift(chain_b, -1),
+            shift(right_part, 1),
+            shift(far_c, 2),
+            shift(left_c, -1),
+            shift(right_c, 1),
+            back_a,
+        )
+    )
+    total_b = add(own_b, summed_b, direct_b)
+    total_c = add(own_c, far_c, left_c, right_c)
+    backs = [back_a, exchange(jnp.concatenate([total_b, total_c], axis=1))]
+    backs = [back.reshape(PACK_ROWS, -1) for back in backs]
     out = combine(attended, backs, gate_probs[0], expert_col, expert_row)
     return out[None]
 

time: 355 us -> 346 us (0.975)
  starting transfers between devices: 68.9 us -> 43.2 us
  waiting for transfers between devices: 152 us -> 168 us
  blocking collectives: 0 us -> 14.9 us
  other arithmetic: 12.5 us -> 4.54 us
    ppermute x18 -> x16, waiting for transfers between devices: 69.8 us -> 86.9 us  [shift(): return lax.ppermute(x, 'z', [(i, (i + by) % 4) for i in range(4)])]
    all_to_all x0 -> x1, blocking collectives: none -> 14.9 us  [exchange(): return lax.all_to_all(x, PLANE, split_axis=0, concat_axis=0, tiled=True)]
    all_to_all x4 -> x2, starting transfers between devices: 29.3 us -> 16.6 us  [exchange(): return lax.all_to_all(x, PLANE, split_axis=0, concat_axis=0, tiled=True)]
    ppermute x6, waiting for transfers between devices: 22.5 us -> 11.6 us  [fetch(): return lax.ppermute(w, ('xh', 'xl', 'core'), moves)]
    ppermute x6, starting transfers between devices: 11.5 us -> 2.3 us  [fetch(): return lax.ppermute(w, ('xh', 'xl', 'core'), moves)]
    all_to_all x4 -> x2, waiting for transfers between devices: 38.5 us -> 45.1 us  [exchange(): return lax.all_to_all(x, PLANE, split_axis=0, concat_axis=0, tiled=True)]
    reshape x3 -> x2, other arithmetic: 6.85 us -> 1.42 us  [exchange(): x = x.reshape(EXPERTS, -1, shape[1])]
    ppermute x18 -> x16, starting transfers between devices: 26.3 us -> 21.5 us  [shift(): return lax.ppermute(x, 'z', [(i, (i + by) % 4) for i in range(4)])]
  transfers between devices with their start and end apart: 35 -> 31, of which waited for: 20 -> 21; matrix products, arithmetic and copies ran while one was open for 10% -> 7% of each run, Pallas kernels for 24% -> 25%
where the time goes in v2:
time: 346 us; the launch traced here: 343 us
  waiting for transfers between devices  168 us (49%)
  Pallas kernels  86.6 us (25%)
  starting transfers between devices  43.2 us (12%)
  local copies, waits for them, and re-layouts  25.7 us (7%)
  blocking collectives  14.9 us (4%)
  other arithmetic  4.54 us (1%)
    ppermute x16, waiting for transfers between devices, shift(): return lax.ppermute(x, 'z', [(i, (i + by) % 4) for i in range(4)])  86.9 us
    all_to_all x2, waiting for transfers between devices, exchange(): return lax.all_to_all(x, PLANE, split_axis=0, concat_axis=0, tiled=True)  45.1 us
    pallas_call x6, Pallas kernels, down(): pl.pallas_call(lambda *refs: down_kernel(count, part, fetches, *refs), gr...  36.7 us
    pallas_call x2, Pallas kernels, gate(): pl.pallas_call(lambda *refs: gate_kernel(count, *refs), grid=(8,), in_spe...  31.4 us
    ppermute x16, starting transfers between devices, shift(): return lax.ppermute(x, 'z', [(i, (i + by) % 4) for i in range(4)])  21.5 us
    slice x6, local copies, waits for them, and re-layouts, cut(): yield lax.slice_in_dim(w, at, at + size, axis=axis)  21.4 us
    all_to_all x2, starting transfers between devices, exchange(): return lax.all_to_all(x, PLANE, split_axis=0, concat_axis=0, tiled=True)  16.6 us
    pallas_call x1, Pallas kernels, attend(): pl.pallas_call(attend_kernel, grid=(KV_HEADS,), in_specs=in_specs, out_sp...  16.1 us
  transfers between devices with their start and end apart: 31, of which 21 were waited for; matrix products, arithmetic and copies ran while one was open for 7% of the time, Pallas kernels for 25%

profile of v2, /device:TPU:36, one launch (start us, length us, event | category | flops | bytes accessed | tf_op | source)
XLA Modules:
  0.0 342.9 jit_solution(12727567450953846409)
XLA Ops:
  6.7 13.0 %collective-permute-done.refs_4_.refs_9_.refs_14_ = bf16[128,2176]{1,0:T(8,128)(2,1)S(1)} collective-permute-done((bf16[128,2176]{1,0:T(8,128)(2,1)S(1)}, bf16[128,2176]{1,0:T(8,128)(2,1)S(1)}, u32[]{:S(2)}, u32[]{:S(2)}) %collective-permute-start) | collective-permute-done | bytes 557088 | tf_op jit(solution)/shard_map/ppermute | solution.py:324
  31.4 3.9 %slice.35 = bf16[672,2560]{1,0:T(8,128)(2,1)} slice(bf16[672,6144]{1,0:T(8,128)(2,1)} %bitcast.31), slice={[0:672], [1536:4096]} | slice | bytes 6881280 | tf_op jit(solution)/shard_map/slice | solution.py:350
  39.0 6.8 %collective-permute-done.2.refs_1_.refs_6_.refs_11_ = bf16[128,2176]{1,0:T(8,128)(2,1)S(1)} collective-permute-done((bf16[128,2176]{1,0:T(8,128)(2,1)S(1)}, bf16[128,2176]{1,0:T(8,128)(2,1)S(1)}, u32[]{:S(2)}, u32[]{:S(2)}) %collective-permute-start.2) | collective-permute-done | bytes 557088 | tf_op jit(solution)/shard_map/ppermute | solution.py:314
  50.7 16.1 %attend.1 = (bf16[128,6144]{1,0:T(8,128)(2,1)}, bf16[256,3840]{1,0:T(8,128)(2,1)}) custom-call(s32[1]{0:T(128)} %bitcast.place_ref, f32[128,1]{1,0:T(8,128)S(1)} %copy.16.doc_ref, s32[128,1]{1,0:T(8,128)S(1)} %add_select_fusion.ecol_ref.refs_3_, s32[1,128]{1,0:T(1,128)S(1)} %and_select_fusion.erow_ref.refs_4_, bf16[128,6144]{1,0:T(8,128)(2,1)} %bitcast.45, ...), custom_call_target="tpu_custom_call" | custom-call | flops 16000000000 | bytes 1000000 | tf_op jit(solution)/shard_map/attend/pallas_call | solution.py:136
  70.7 9.6 %all-to-all-start = ((bf16[16,16,3840]{2,1,0:T(8,128)(2,1)}), bf16[16,16,3840]{2,1,0:T(8,128)(2,1)S(1)}, u32[]{:S(2)}, u32[]{:S(2)}) async-start(bf16[16,16,3840]{2,1,0:T(8,128)(2,1)} %bitcast.43), calls=%async_computation | async-start | bytes 3932160 | tf_op jit(solution)/shard_map/all_to_all | solution.py:371
  80.3 4.6 %slice.37 = bf16[336,6144]{1,0:T(8,128)(2,1)} slice(bf16[672,6144]{1,0:T(8,128)(2,1)} %bitcast.35), slice={[336:672], [0:6144]} | slice | bytes 8257536 | tf_op jit(solution)/shard_map/slice | solution.py:350
  84.9 23.1 %all-to-all-done = bf16[16,16,3840]{2,1,0:T(8,128)(2,1)S(1)} async-done(((bf16[16,16,3840]{2,1,0:T(8,128)(2,1)}), bf16[16,16,3840]{2,1,0:T(8,128)(2,1)S(1)}, u32[]{:S(2)}, u32[]{:S(2)}) %all-to-all-start) | async-done | bytes 1966112 | tf_op jit(solution)/shard_map/all_to_all | solution.py:371
  110.2 42.9 %collective-permute-done.8.refs_0_.refs_1_ = bf16[256,3840]{1,0:T(8,128)(2,1)S(1)} collective-permute-done((bf16[256,3840]{1,0:T(8,128)(2,1)S(1)}, bf16[256,3840]{1,0:T(8,128)(2,1)S(1)}, u32[]{:S(2)}, u32[]{:S(2)}) %collective-permute-start.8) | collective-permute-done | bytes 1966112 | tf_op jit(solution)/shard_map/ppermute | solution.py:314
  162.6 19.8 %gate.2.refs_0_ = bf16[2,480,672]{2,1,0:T(8,128)(2,1)S(1)} custom-call(bf16[256,3840]{1,0:T(8,128)(2,1)} %copy-done.7, bf16[256,3840]{1,0:T(8,128)(2,1)} %copy-done.7, bf16[256,3840]{1,0:T(8,128)(2,1)} %copy-done.8, bf16[256,3840]{1,0:T(8,128)(2,1)} %copy-done.8, bf16[256,3840]{1,0:T(8,128)(2,1)} %bitcast.41, bf16[256,3840]{1,0:T(8,128)(2,1)} %bitcast.42, ...), custom_call_target="tpu_custom_call" | custom-call | flops 20000000000 | bytes 1000000 | tf_op jit(solution)/shard_map/gate/pallas_call | solution.py:204
  184.5 11.6 %gate.3.refs_0_ = bf16[2,160,672]{2,1,0:T(8,128)(2,1)S(1)} custom-call(bf16[128,3840]{1,0:T(8,128)(2,1)S(1)} %collective-permute-done.12.refs_0_, bf16[128,3840]{1,0:T(8,128)(2,1)S(1)} %collective-permute-done.13.refs_1_, bf16[208,6144]{1,0:T(8,128)(2,1)} %collective-permute-done.1.refs_6_.refs_2_, bf16[128,6144]{1,0:T(8,128)(2,1)} %collective-permute-done.5.refs_7_.refs_3_, ...), custom_call_target="tpu_custom_call" | custom-call | flops 12000000000 | bytes 1000000 | tf_op jit(solution)/shard_map/gate/pallas_call | solution.py:204
  197.4 4.1 %down.6 = bf16[128,1920]{1,0:T(8,128)(2,1)S(1)} custom-call(bf16[2,160,672]{2,1,0:T(8,128)(2,1)S(1)} %gate.3.refs_0_, bf16[672,1536]{1,0:T(8,128)(2,1)S(1)} %collective-permute-done.14.refs_1_, bf16[672,1536]{1,0:T(8,128)(2,1)} %copy-done.11), custom_call_target="tpu_custom_call" | custom-call | flops 4000000000 | bytes 1000000 | tf_op jit(solution)/shard_map/down/pallas_call | solution.py:266
  203.2 6.7 %down.7 = (bf16[128,1920]{1,0:T(8,128)(2,1)S(1)}, bf16[128,1920]{1,0:T(8,128)(2,1)S(1)}, bf16[128,1920]{1,0:T(8,128)(2,1)S(1)}) custom-call(bf16[2,480,672]{2,1,0:T(8,128)(2,1)S(1)} %gate.2.refs_0_, bf16[672,1536]{1,0:T(8,128)(2,1)} %copy-done.1, bf16[672,1536]{1,0:T(8,128)(2,1)} %copy-done.11), custom_call_target="tpu_custom_call" | custom-call | flops 8000000000 | bytes 1000000 | tf_op jit(solution)/shard_map/down/pallas_call | solution.py:266
  210.4 5.2 %collective-permute-done.16 = bf16[128,1920]{1,0:T(8,128)(2,1)S(1)} collective-permute-done((bf16[128,1920]{1,0:T(8,128)(2,1)S(1)}, bf16[128,1920]{1,0:T(8,128)(2,1)S(1)}, u32[]{:S(2)}, u32[]{:S(2)}) %collective-permute-start.16) | collective-permute-done | bytes 491552 | tf_op jit(solution)/shard_map/ppermute | solution.py:314
  215.6 8.5 %collective-permute-done.17 = bf16[128,1920]{1,0:T(8,128)(2,1)S(1)} collective-permute-done((bf16[128,1920]{1,0:T(8,128)(2,1)S(1)}, bf16[128,1920]{1,0:T(8,128)(2,1)S(1)}, u32[]{:S(2)}, u32[]{:S(2)}) %collective-permute-start.17) | collective-permute-done | bytes 491552 | tf_op jit(solution)/shard_map/ppermute | solution.py:314
  225.1 5.4 %collective-permute-done.20.refs_2_ = bf16[672,2560]{1,0:T(8,128)(2,1)} collective-permute-done((bf16[672,2560]{1,0:T(8,128)(2,1)}, bf16[672,2560]{1,0:T(8,128)(2,1)}, u32[]{:S(2)}, u32[]{:S(2)}) %collective-permute-start.20) | collective-permute-done | bytes 3440672 | tf_op jit(solution)/shard_map/ppermute | solution.py:345
  230.5 5.3 %down.8 = bf16[128,3200]{1,0:T(8,128)(2,1)S(1)} custom-call(bf16[2,160,672]{2,1,0:T(8,128)(2,1)S(1)} %gate.3.refs_0_, bf16[672,2560]{1,0:T(8,128)(2,1)} %collective-permute-done.18.refs_1_, bf16[672,2560]{1,0:T(8,128)(2,1)} %collective-permute-done.20.refs_2_), custom_call_target="tpu_custom_call" | custom-call | flops 4000000000 | bytes 1000000 | tf_op jit(solution)/shard_map/down/pallas_call | solution.py:266
  238.1 9.3 %down.9 = (bf16[128,3200]{1,0:T(8,128)(2,1)S(1)}, bf16[128,3200]{1,0:T(8,128)(2,1)S(1)}, bf16[128,3200]{1,0:T(8,128)(2,1)S(1)}) custom-call(bf16[2,480,672]{2,1,0:T(8,128)(2,1)S(1)} %gate.2.refs_0_, bf16[672,2560]{1,0:T(8,128)(2,1)} %collective-permute-done.18.refs_1_, bf16[672,2560]{1,0:T(8,128)(2,1)} %collective-permute-done.20.refs_2_), custom_call_target="tpu_custom_call" | custom-call | flops 8000000000 | bytes 1000000 | tf_op jit(solution)/shard_map/down/pallas_call | solution.py:266
  250.9 5.9 %collective-permute-done.22.refs_1_ = bf16[672,2048]{1,0:T(8,128)(2,1)S(1)} collective-permute-done((bf16[672,2048]{1,0:T(8,128)(2,1)}, bf16[672,2048]{1,0:T(8,128)(2,1)S(1)}, u32[]{:S(2)}, u32[]{:S(2)}) %collective-permute-start.22) | collective-permute-done | bytes 2752544 | tf_op jit(solution)/shard_map/ppermute | solution.py:342
  262.3 4.3 %down.10 = bf16[128,2560]{1,0:T(8,128)(2,1)S(1)} custom-call(bf16[2,160,672]{2,1,0:T(8,128)(2,1)S(1)} %gate.3.refs_0_, bf16[672,2048]{1,0:T(8,128)(2,1)S(1)} %collective-permute-done.22.refs_1_, bf16[672,2048]{1,0:T(8,128)(2,1)} %collective-permute-done.25.refs_2_), custom_call_target="tpu_custom_call" | custom-call | flops 3000000000 | bytes 1000000 | tf_op jit(solution)/shard_map/down/pallas_call | solution.py:266
  269.6 7.0 %down.11 = (bf16[128,2560]{1,0:T(8,128)(2,1)S(1)}, bf16[128,2560]{1,0:T(8,128)(2,1)S(1)}, bf16[128,2560]{1,0:T(8,128)(2,1)S(1)}) custom-call(bf16[2,480,672]{2,1,0:T(8,128)(2,1)S(1)} %gate.2.refs_0_, bf16[672,2048]{1,0:T(8,128)(2,1)} %copy-done, bf16[672,2048]{1,0:T(8,128)(2,1)} %collective-permute-done.25.refs_2_), custom_call_target="tpu_custom_call" | custom-call | flops 6000000000 | bytes 1000000 | tf_op jit(solution)/shard_map/down/pallas_call | solution.py:266
  278.9 14.9 %all_to_all.15 = bf16[16,8,1920]{2,1,0:T(8,128)(2,1)S(1)} all-to-all(bf16[16,8,1920]{2,1,0:T(8,128)(2,1)S(1)} %fusion), channel_id=1, replica_groups=mesh['xh'=2,'z'=4,'xl'=2,'y'=4,'core'=2] {'xl','y','xh'}, dimensions={0} | all-to-all | bytes 983040 | tf_op jit(solution)/shard_map/all_to_all | solution.py:371
  294.2 12.7 %collective-permute-done.27 = bf16[128,2560]{1,0:T(8,128)(2,1)S(1)} collective-permute-done((bf16[128,2560]{1,0:T(8,128)(2,1)S(1)}, bf16[128,2560]{1,0:T(8,128)(2,1)S(1)}, u32[]{:S(2)}, u32[]{:S(2)}) %collective-permute-start.27) | collective-permute-done | bytes 655392 | tf_op jit(solution)/shard_map/ppermute | solution.py:314
  309.9 7.0 %all-to-all-start.2 = ((bf16[16,8,5760]{2,1,0:T(8,128)(2,1)}), bf16[16,8,5760]{2,1,0:T(8,128)(2,1)S(1)}, u32[]{:S(2)}, u32[]{:S(2)}) async-start(bf16[16,8,5760]{2,1,0:T(8,128)(2,1)} %maximum_bitcast_fusion), calls=%async_computation.2 | async-start | bytes 2949120 | tf_op jit(solution)/shard_map/all_to_all | solution.py:371
  317.0 22.1 %all-to-all-done.2 = bf16[16,8,5760]{2,1,0:T(8,128)(2,1)S(1)} async-done(((bf16[16,8,5760]{2,1,0:T(8,128)(2,1)}), bf16[16,8,5760]{2,1,0:T(8,128)(2,1)S(1)}, u32[]{:S(2)}, u32[]{:S(2)}) %all-to-all-start.2) | async-done | bytes 1474592 | tf_op jit(solution)/shard_map/all_to_all | solution.py:371
  (100 shorter events, 73.0 us)
Async XLA Ops:
  1.9 17.8 %collective-permute-start = (bf16[128,2176]{1,0:T(8,128)(2,1)S(1)}, bf16[128,2176]{1,0:T(8,128)(2,1)S(1)}, u32[]{:S(2)}, u32[]{:S(2)}) collective-permute-start(bf16[128,2176]{1,0:T(8,128)(2,1)S(1)} %pad_maximum_fusion.refs_0_.refs_5_.refs_10_), channel_id=1, source_target_pairs={{0,64},{1,65},{2,66},{3,67},{4,68},{5,69},{6,70},{7,71},{8,72},{9,... | collective-permute-start | bytes 1671176 | tf_op jit(solution)/shard_map/ppermute | solution.py:324
  19.6 30.7 %collective-permute-start.1 = (bf16[208,6144]{1,0:T(8,128)(2,1)}, bf16[208,6144]{1,0:T(8,128)(2,1)}, u32[]{:S(2)}, u32[]{:S(2)}) collective-permute-start(bf16[208,6144]{1,0:T(8,128)(2,1)} %slice.32), channel_id=1, source_target_pairs={{0,8},{1,72},{8,0},{9,64},{64,9},{65,73},{72,1},{73,65},{2,10},{3,... | collective-permute-start | bytes 7667720 | tf_op jit(solution)/shard_map/ppermute | solution.py:342
  19.9 25.9 %collective-permute-start.2 = (bf16[128,2176]{1,0:T(8,128)(2,1)S(1)}, bf16[128,2176]{1,0:T(8,128)(2,1)S(1)}, u32[]{:S(2)}, u32[]{:S(2)}) collective-permute-start(bf16[128,2176]{1,0:T(8,128)(2,1)S(1)} %get-tuple-element.133), channel_id=1, source_target_pairs={{0,16},{16,32},{32,48},{48,0},{1,17},{17,33},{33,49},{49,1},{2,18}... | collective-permute-start | bytes 1671176 | tf_op jit(solution)/shard_map/ppermute | solution.py:314
  21.9 23.9 %collective-permute-start.3 = (bf16[128,2176]{1,0:T(8,128)(2,1)S(1)}, bf16[128,2176]{1,0:T(8,128)(2,1)S(1)}, u32[]{:S(2)}, u32[]{:S(2)}) collective-permute-start(bf16[128,2176]{1,0:T(8,128)(2,1)S(1)} %get-tuple-element.132), channel_id=1, source_target_pairs={{0,32},{16,48},{32,0},{48,16},{1,33},{17,49},{33,1},{49,17},{2,34}... | collective-permute-start | bytes 1671176 | tf_op jit(solution)/shard_map/ppermute | solution.py:314
  23.1 26.1 %collective-permute-start.4 = (bf16[128,2176]{1,0:T(8,128)(2,1)S(1)}, bf16[128,2176]{1,0:T(8,128)(2,1)S(1)}, u32[]{:S(2)}, u32[]{:S(2)}) collective-permute-start(bf16[128,2176]{1,0:T(8,128)(2,1)S(1)} %get-tuple-element.131), channel_id=1, source_target_pairs={{0,48},{16,0},{32,16},{48,32},{1,49},{17,1},{33,17},{49,33},{2,50}... | collective-permute-start | bytes 1671176 | tf_op jit(solution)/shard_map/ppermute | solution.py:314
  50.3 20.4 %collective-permute-start.6 = (bf16[208,6144]{1,0:T(8,128)(2,1)}, bf16[208,6144]{1,0:T(8,128)(2,1)}, u32[]{:S(2)}, u32[]{:S(2)}) collective-permute-start(bf16[208,6144]{1,0:T(8,128)(2,1)} %collective-permute-done.1.refs_6_.refs_2_), channel_id=1, source_target_pairs={{0,1},{1,0},{2,3},{3,2},{4,5},{5,4},{6,7},{7,6},{8,9},{9,8},{10,11... | collective-permute-start | bytes 7667720 | tf_op jit(solution)/shard_map/ppermute | solution.py:345
  50.5 20.2 %collective-permute-start.5 = (bf16[128,6144]{1,0:T(8,128)(2,1)}, bf16[128,6144]{1,0:T(8,128)(2,1)}, u32[]{:S(2)}, u32[]{:S(2)}) collective-permute-start(bf16[128,6144]{1,0:T(8,128)(2,1)} %slice.33), channel_id=1, source_target_pairs={{0,8},{1,72},{8,0},{9,64},{64,9},{65,73},{72,1},{73,65},{2,10},{3,... | collective-permute-start | bytes 4718600 | tf_op jit(solution)/shard_map/ppermute | solution.py:342
  70.7 37.3 %all-to-all-start = ((bf16[16,16,3840]{2,1,0:T(8,128)(2,1)}), bf16[16,16,3840]{2,1,0:T(8,128)(2,1)S(1)}, u32[]{:S(2)}, u32[]{:S(2)}) async-start(bf16[16,16,3840]{2,1,0:T(8,128)(2,1)} %bitcast.43), calls=%async_computation | async-start | bytes 3932160 | tf_op jit(solution)/shard_map/all_to_all | solution.py:371
  108.0 47.4 %collective-permute-start.10 = (bf16[336,6144]{1,0:T(8,128)(2,1)}, bf16[336,6144]{1,0:T(8,128)(2,1)S(1)}, u32[]{:S(2)}, u32[]{:S(2)}) collective-permute-start(bf16[336,6144]{1,0:T(8,128)(2,1)} %slice.37), channel_id=1, source_target_pairs={{0,8},{1,72},{8,0},{9,64},{64,9},{65,73},{72,1},{73,65},{2,10},{3,... | collective-permute-start | bytes 12386312 | tf_op jit(solution)/shard_map/ppermute | solution.py:342
  108.2 45.0 %collective-permute-start.8 = (bf16[256,3840]{1,0:T(8,128)(2,1)S(1)}, bf16[256,3840]{1,0:T(8,128)(2,1)S(1)}, u32[]{:S(2)}, u32[]{:S(2)}) collective-permute-start(bf16[256,3840]{1,0:T(8,128)(2,1)S(1)} %bitcast.39), channel_id=1, source_target_pairs={{0,16},{16,32},{32,48},{48,0},{1,17},{17,33},{33,49},{49,1},{2,18}... | collective-permute-start | bytes 5898248 | tf_op jit(solution)/shard_map/ppermute | solution.py:314
  110.1 44.7 %collective-permute-start.9 = (bf16[256,3840]{1,0:T(8,128)(2,1)S(1)}, bf16[256,3840]{1,0:T(8,128)(2,1)S(1)}, u32[]{:S(2)}, u32[]{:S(2)}) collective-permute-start(bf16[256,3840]{1,0:T(8,128)(2,1)S(1)} %bitcast.40), channel_id=1, source_target_pairs={{0,48},{16,0},{32,16},{48,32},{1,49},{17,1},{33,17},{49,33},{2,50}... | collective-permute-start | bytes 5898248 | tf_op jit(solution)/shard_map/ppermute | solution.py:314
  155.5 27.6 %collective-permute-start.14 = (bf16[672,1536]{1,0:T(8,128)(2,1)S(1)}, bf16[672,1536]{1,0:T(8,128)(2,1)S(1)}, u32[]{:S(2)}, u32[]{:S(2)}) collective-permute-start(bf16[672,1536]{1,0:T(8,128)(2,1)S(1)} %copy-done.5), channel_id=1, source_target_pairs={{0,8},{1,72},{8,0},{9,64},{64,9},{65,73},{72,1},{73,65},{2,10},{3,... | collective-permute-start | bytes 6193160 | tf_op jit(solution)/shard_map/ppermute | solution.py:342
  156.2 26.3 %collective-permute-start.12 = (bf16[128,3840]{1,0:T(8,128)(2,1)S(1)}, bf16[128,3840]{1,0:T(8,128)(2,1)S(1)}, u32[]{:S(2)}, u32[]{:S(2)}) collective-permute-start(bf16[128,3840]{1,0:T(8,128)(2,1)S(1)} %slice.30), channel_id=1, source_target_pairs={{0,16},{16,32},{32,48},{48,0},{1,17},{17,33},{33,49},{49,1},{2,18}... | collective-permute-start | bytes 2949128 | tf_op jit(solution)/shard_map/ppermute | solution.py:314
  159.2 23.9 %collective-permute-start.13 = (bf16[128,3840]{1,0:T(8,128)(2,1)}, bf16[128,3840]{1,0:T(8,128)(2,1)S(1)}, u32[]{:S(2)}, u32[]{:S(2)}) collective-permute-start(bf16[128,3840]{1,0:T(8,128)(2,1)} %slice.31), channel_id=1, source_target_pairs={{0,48},{16,0},{32,16},{48,32},{1,49},{17,1},{33,17},{49,33},{2,50}... | collective-permute-start | bytes 2949128 | tf_op jit(solution)/shard_map/ppermute | solution.py:314
  183.9 40.2 %collective-permute-start.18 = (bf16[672,2560]{1,0:T(8,128)(2,1)S(1)}, bf16[672,2560]{1,0:T(8,128)(2,1)}, u32[]{:S(2)}, u32[]{:S(2)}) collective-permute-start(bf16[672,2560]{1,0:T(8,128)(2,1)S(1)} %copy-done.3), channel_id=1, source_target_pairs={{0,8},{1,72},{8,0},{9,64},{64,9},{65,73},{72,1},{73,65},{2,10},{3,... | collective-permute-start | bytes 10321928 | tf_op jit(solution)/shard_map/ppermute | solution.py:342
  224.2 32.7 %collective-permute-start.22 = (bf16[672,2048]{1,0:T(8,128)(2,1)}, bf16[672,2048]{1,0:T(8,128)(2,1)S(1)}, u32[]{:S(2)}, u32[]{:S(2)}) collective-permute-start(bf16[672,2048]{1,0:T(8,128)(2,1)} %slice.36), channel_id=1, source_target_pairs={{0,8},{1,72},{8,0},{9,64},{64,9},{65,73},{72,1},{73,65},{2,10},{3,... | collective-permute-start | bytes 8257544 | tf_op jit(solution)/shard_map/ppermute | solution.py:342
  235.8 21.1 %collective-permute-start.21 = (bf16[128,3200]{1,0:T(8,128)(2,1)S(1)}, bf16[128,3200]{1,0:T(8,128)(2,1)S(1)}, u32[]{:S(2)}, u32[]{:S(2)}) collective-permute-start(bf16[128,3200]{1,0:T(8,128)(2,1)S(1)} %down.8), channel_id=1, source_target_pairs={{0,48},{16,0},{32,16},{48,32},{1,49},{17,1},{33,17},{49,33},{2,50}... | collective-permute-start | bytes 2457608 | tf_op jit(solution)/shard_map/ppermute | solution.py:314
  236.3 14.6 %collective-permute-start.19 = (bf16[128,1920]{1,0:T(8,128)(2,1)S(1)}, bf16[128,1920]{1,0:T(8,128)(2,1)S(1)}, u32[]{:S(2)}, u32[]{:S(2)}) collective-permute-start(bf16[128,1920]{1,0:T(8,128)(2,1)S(1)} %add_convert_fusion.4), channel_id=1, source_target_pairs={{0,16},{16,32},{32,48},{48,0},{1,17},{17,33},{33,49},{49,1},{2,18}... | collective-permute-start | bytes 1474568 | tf_op jit(solution)/shard_map/ppermute | solution.py:314
  257.6 36.1 %collective-permute-start.23 = (bf16[128,3200]{1,0:T(8,128)(2,1)S(1)}, bf16[128,3200]{1,0:T(8,128)(2,1)S(1)}, u32[]{:S(2)}, u32[]{:S(2)}) collective-permute-start(bf16[128,3200]{1,0:T(8,128)(2,1)S(1)} %add_convert_fusion.1), channel_id=1, source_target_pairs={{0,48},{16,0},{32,16},{48,32},{1,49},{17,1},{33,17},{49,33},{2,50}... | collective-permute-start | bytes 2457608 | tf_op jit(solution)/shard_map/ppermute | solution.py:314
  258.0 35.8 %collective-permute-start.24 = (bf16[128,3200]{1,0:T(8,128)(2,1)S(1)}, bf16[128,3200]{1,0:T(8,128)(2,1)S(1)}, u32[]{:S(2)}, u32[]{:S(2)}) collective-permute-start(bf16[128,3200]{1,0:T(8,128)(2,1)S(1)} %get-tuple-element.115), channel_id=1, source_target_pairs={{0,16},{16,32},{32,48},{48,0},{1,17},{17,33},{33,49},{49,1},{2,18}... | collective-permute-start | bytes 2457608 | tf_op jit(solution)/shard_map/ppermute | solution.py:314
  266.6 27.6 %collective-permute-start.26 = (bf16[128,2560]{1,0:T(8,128)(2,1)S(1)}, bf16[128,2560]{1,0:T(8,128)(2,1)S(1)}, u32[]{:S(2)}, u32[]{:S(2)}) collective-permute-start(bf16[128,2560]{1,0:T(8,128)(2,1)S(1)} %down.10), channel_id=1, source_target_pairs={{0,32},{16,48},{32,0},{48,16},{1,33},{17,49},{33,1},{49,17},{2,34}... | collective-permute-start | bytes 1966088 | tf_op jit(solution)/shard_map/ppermute | solution.py:314
  276.6 30.3 %collective-permute-start.27 = (bf16[128,2560]{1,0:T(8,128)(2,1)S(1)}, bf16[128,2560]{1,0:T(8,128)(2,1)S(1)}, u32[]{:S(2)}, u32[]{:S(2)}) collective-permute-start(bf16[128,2560]{1,0:T(8,128)(2,1)S(1)} %get-tuple-element.118), channel_id=1, source_target_pairs={{0,48},{16,0},{32,16},{48,32},{1,49},{17,1},{33,17},{49,33},{2,50}... | collective-permute-start | bytes 1966088 | tf_op jit(solution)/shard_map/ppermute | solution.py:314
  277.7 30.4 %collective-permute-start.28 = (bf16[128,2560]{1,0:T(8,128)(2,1)S(1)}, bf16[128,2560]{1,0:T(8,128)(2,1)S(1)}, u32[]{:S(2)}, u32[]{:S(2)}) collective-permute-start(bf16[128,2560]{1,0:T(8,128)(2,1)S(1)} %get-tuple-element.119), channel_id=1, source_target_pairs={{0,16},{16,32},{32,48},{48,0},{1,17},{17,33},{33,49},{49,1},{2,18}... | collective-permute-start | bytes 1966088 | tf_op jit(solution)/shard_map/ppermute | solution.py:314
  309.9 29.2 %all-to-all-start.2 = ((bf16[16,8,5760]{2,1,0:T(8,128)(2,1)}), bf16[16,8,5760]{2,1,0:T(8,128)(2,1)S(1)}, u32[]{:S(2)}, u32[]{:S(2)}) async-start(bf16[16,8,5760]{2,1,0:T(8,128)(2,1)} %maximum_bitcast_fusion), calls=%async_computation.2 | async-start | bytes 2949120 | tf_op jit(solution)/shard_map/all_to_all | solution.py:371
  (20 other events, 265.2 us)

commit v3 on v2

--- a/solution.py
+++ b/solution.py
@@ -170,19 +170,22 @@
     def _():
         pre[...] = jnp.zeros_like(pre)
 
-    for n in range(8):
+    for n in range(4):
 
         @pl.when(step == n)
         def _(n=n):
-            h, o = n // FOLD, n % FOLD
+            h = n // 2
             m = iota((EXPERTS * 2, PACK_ROWS), 0)
             c = iota((EXPERTS * 2, PACK_ROWS), 1)
-            pick = (c == (m // 2) * MAIN + 2 * o + m % 2).astype(F32).astype(BF)
-            for i in range(count):
-                pack = packs[2 * i + h]
-                lo = i * BLOCK_ROWS
-                rows[lo : lo + PACK_ROWS, :] = pack[:, o * GW : (o + 1) * GW]
-                rows[lo + PACK_ROWS : lo + BLOCK_ROWS, :] = dot(pick, pack[:, HALF:]).astype(BF)
+            for p in range(2):
+                o = 2 * (n % 2) + p
+                cols = slice(p * GW, (p + 1) * GW)
+                pick = (c == (m // 2) * MAIN + 2 * o + m % 2).astype(F32).astype(BF)
+                for i in range(count):
+                    pack = packs[2 * i + h]
+                    lo = i * BLOCK_ROWS
+                    rows[lo : lo + PACK_ROWS, cols] = pack[:, o * GW : (o + 1) * GW]
+                    rows[lo + PACK_ROWS : lo + BLOCK_ROWS, cols] = dot(pick, pack[:, HALF:]).astype(BF)
 
     x = rows[...]
     for n, w in enumerate(w_refs):
@@ -190,7 +193,7 @@
         units = slice(at, at + UNITS[n % len(UNITS)])
         pre[n // len(UNITS), units, :] += dot_t(w[...], x)
 
-    @pl.when(step == 7)
+    @pl.when(step == 3)
     def _():
         for s in range(2):
             x = pre[s]
@@ -203,12 +206,12 @@
     pack_specs = [pl.BlockSpec((PACK_ROWS, HALF + GW), lambda i, at=at: (at, 0)) for _, at in packs]
     return pl.pallas_call(
         lambda *refs: gate_kernel(count, *refs),
-        grid=(8,),
+        grid=(4,),
         in_specs=pack_specs
-        + [pl.BlockSpec((units, GW), lambda i: (0, i)) for units in UNITS * 2],
+        + [pl.BlockSpec((units, 2 * GW), lambda i: (0, i)) for units in UNITS * 2],
         out_specs=pl.BlockSpec((2, rows, UNIT), lambda i: (0, 0, 0)),
         out_shape=jax.ShapeDtypeStruct((2, rows, UNIT), BF),
-        scratch_shapes=[pltpu.VMEM((2, UNIT, rows), F32), pltpu.VMEM((rows, GW), BF)],
+        scratch_shapes=[pltpu.VMEM((2, UNIT, rows), F32), pltpu.VMEM((rows, 2 * GW), BF)],
         compiler_params=pltpu.CompilerParams(vmem_limit_bytes=VMEM),
         cost_estimate=cost(8 + rows // 40),
         name="gate",

time: 346 us -> 345 us (level)
  Pallas kernels: 86.6 us -> 83 us
    pallas_call x2, Pallas kernels: 31.4 us -> 27.8 us  [gate(): pl.pallas_call(lambda *refs: gate_kernel(count, *refs), grid=(4,), in_spe...]
  transfers between devices with their start and end apart: 31 -> 31, of which waited for: 21 -> 22; matrix products, arithmetic and copies ran while one was open for 7% -> 7% of each run, Pallas kernels for 25% -> 24%
where the time goes in v3:
time: 345 us; the launch traced here: 343 us
  waiting for transfers between devices  171 us (50%)
  Pallas kernels  83 us (24%)
  starting transfers between devices  43.1 us (12%)
  local copies, waits for them, and re-layouts  25.7 us (7%)
  blocking collectives  14.7 us (4%)
  other arithmetic  4.54 us (1%)
    ppermute x16, waiting for transfers between devices, shift(): return lax.ppermute(x, 'z', [(i, (i + by) % 4) for i in range(4)])  88.8 us
    all_to_all x2, waiting for transfers between devices, exchange(): return lax.all_to_all(x, PLANE, split_axis=0, concat_axis=0, tiled=True)  45.1 us
    pallas_call x6, Pallas kernels, down(): pl.pallas_call(lambda *refs: down_kernel(count, part, fetches, *refs), gr...  36.7 us
    pallas_call x2, Pallas kernels, gate(): pl.pallas_call(lambda *refs: gate_kernel(count, *refs), grid=(4,), in_spe...  27.8 us
    slice x6, local copies, waits for them, and re-layouts, cut(): yield lax.slice_in_dim(w, at, at + size, axis=axis)  21.4 us
    ppermute x16, starting transfers between devices, shift(): return lax.ppermute(x, 'z', [(i, (i + by) % 4) for i in range(4)])  21.2 us
    all_to_all x2, starting transfers between devices, exchange(): return lax.all_to_all(x, PLANE, split_axis=0, concat_axis=0, tiled=True)  16.3 us
    pallas_call x1, Pallas kernels, attend(): pl.pallas_call(attend_kernel, grid=(KV_HEADS,), in_specs=in_specs, out_sp...  16.1 us
  transfers between devices with their start and end apart: 31, of which 22 were waited for; matrix products, arithmetic and copies ran while one was open for 7% of the time, Pallas kernels for 24%

profile of v3, /device:TPU:36, one launch (start us, length us, event | category | flops | bytes accessed | tf_op | source)
XLA Modules:
  0.0 342.5 jit_solution(5675749554012106879)
XLA Ops:
  6.7 13.0 %collective-permute-done.refs_4_.refs_9_.refs_14_ = bf16[128,2176]{1,0:T(8,128)(2,1)S(1)} collective-permute-done((bf16[128,2176]{1,0:T(8,128)(2,1)S(1)}, bf16[128,2176]{1,0:T(8,128)(2,1)S(1)}, u32[]{:S(2)}, u32[]{:S(2)}) %collective-permute-start) | collective-permute-done | bytes 557088 | tf_op jit(solution)/shard_map/ppermute | solution.py:327
  31.4 3.9 %slice.35 = bf16[672,2560]{1,0:T(8,128)(2,1)} slice(bf16[672,6144]{1,0:T(8,128)(2,1)} %bitcast.31), slice={[0:672], [1536:4096]} | slice | bytes 6881280 | tf_op jit(solution)/shard_map/slice | solution.py:353
  39.0 6.8 %collective-permute-done.2.refs_1_.refs_6_.refs_11_ = bf16[128,2176]{1,0:T(8,128)(2,1)S(1)} collective-permute-done((bf16[128,2176]{1,0:T(8,128)(2,1)S(1)}, bf16[128,2176]{1,0:T(8,128)(2,1)S(1)}, u32[]{:S(2)}, u32[]{:S(2)}) %collective-permute-start.2) | collective-permute-done | bytes 557088 | tf_op jit(solution)/shard_map/ppermute | solution.py:317
  50.7 16.1 %attend.1 = (bf16[128,6144]{1,0:T(8,128)(2,1)}, bf16[256,3840]{1,0:T(8,128)(2,1)}) custom-call(s32[1]{0:T(128)} %bitcast.place_ref, f32[128,1]{1,0:T(8,128)S(1)} %copy.16.doc_ref, s32[128,1]{1,0:T(8,128)S(1)} %add_select_fusion.ecol_ref.refs_3_, s32[1,128]{1,0:T(1,128)S(1)} %and_select_fusion.erow_ref.refs_4_, bf16[128,6144]{1,0:T(8,128)(2,1)} %bitcast.45, ...), custom_call_target="tpu_custom_call" | custom-call | flops 16000000000 | bytes 1000000 | tf_op jit(solution)/shard_map/attend/pallas_call | solution.py:136
  70.7 9.6 %all-to-all-start = ((bf16[16,16,3840]{2,1,0:T(8,128)(2,1)}), bf16[16,16,3840]{2,1,0:T(8,128)(2,1)S(1)}, u32[]{:S(2)}, u32[]{:S(2)}) async-start(bf16[16,16,3840]{2,1,0:T(8,128)(2,1)} %bitcast.43), calls=%async_computation | async-start | bytes 3932160 | tf_op jit(solution)/shard_map/all_to_all | solution.py:374
  80.3 4.6 %slice.37 = bf16[336,6144]{1,0:T(8,128)(2,1)} slice(bf16[672,6144]{1,0:T(8,128)(2,1)} %bitcast.35), slice={[336:672], [0:6144]} | slice | bytes 8257536 | tf_op jit(solution)/shard_map/slice | solution.py:353
  84.9 23.1 %all-to-all-done = bf16[16,16,3840]{2,1,0:T(8,128)(2,1)S(1)} async-done(((bf16[16,16,3840]{2,1,0:T(8,128)(2,1)}), bf16[16,16,3840]{2,1,0:T(8,128)(2,1)S(1)}, u32[]{:S(2)}, u32[]{:S(2)}) %all-to-all-start) | async-done | bytes 1966112 | tf_op jit(solution)/shard_map/all_to_all | solution.py:374
  110.2 42.9 %collective-permute-done.8.refs_0_.refs_1_ = bf16[256,3840]{1,0:T(8,128)(2,1)S(1)} collective-permute-done((bf16[256,3840]{1,0:T(8,128)(2,1)S(1)}, bf16[256,3840]{1,0:T(8,128)(2,1)S(1)}, u32[]{:S(2)}, u32[]{:S(2)}) %collective-permute-start.8) | collective-permute-done | bytes 1966112 | tf_op jit(solution)/shard_map/ppermute | solution.py:317
  162.6 18.3 %gate.2.refs_0_ = bf16[2,480,672]{2,1,0:T(8,128)(2,1)S(1)} custom-call(bf16[256,3840]{1,0:T(8,128)(2,1)} %copy-done.7, bf16[256,3840]{1,0:T(8,128)(2,1)} %copy-done.7, bf16[256,3840]{1,0:T(8,128)(2,1)} %copy-done.8, bf16[256,3840]{1,0:T(8,128)(2,1)} %copy-done.8, bf16[256,3840]{1,0:T(8,128)(2,1)} %bitcast.41, bf16[256,3840]{1,0:T(8,128)(2,1)} %bitcast.42, ...), custom_call_target="tpu_custom_call" | custom-call | flops 20000000000 | bytes 1000000 | tf_op jit(solution)/shard_map/gate/pallas_call | solution.py:207
  184.5 9.5 %gate.3.refs_0_ = bf16[2,160,672]{2,1,0:T(8,128)(2,1)S(1)} custom-call(bf16[128,3840]{1,0:T(8,128)(2,1)S(1)} %collective-permute-done.12.refs_0_, bf16[128,3840]{1,0:T(8,128)(2,1)S(1)} %collective-permute-done.13.refs_1_, bf16[208,6144]{1,0:T(8,128)(2,1)} %collective-permute-done.1.refs_6_.refs_2_, bf16[128,6144]{1,0:T(8,128)(2,1)} %collective-permute-done.5.refs_7_.refs_3_, ...), custom_call_target="tpu_custom_call" | custom-call | flops 12000000000 | bytes 1000000 | tf_op jit(solution)/shard_map/gate/pallas_call | solution.py:207
  195.3 4.1 %down.6 = bf16[128,1920]{1,0:T(8,128)(2,1)S(1)} custom-call(bf16[2,160,672]{2,1,0:T(8,128)(2,1)S(1)} %gate.3.refs_0_, bf16[672,1536]{1,0:T(8,128)(2,1)S(1)} %collective-permute-done.14.refs_1_, bf16[672,1536]{1,0:T(8,128)(2,1)} %copy-done.11), custom_call_target="tpu_custom_call" | custom-call | flops 4000000000 | bytes 1000000 | tf_op jit(solution)/shard_map/down/pallas_call | solution.py:269
  201.1 6.7 %down.7 = (bf16[128,1920]{1,0:T(8,128)(2,1)S(1)}, bf16[128,1920]{1,0:T(8,128)(2,1)S(1)}, bf16[128,1920]{1,0:T(8,128)(2,1)S(1)}) custom-call(bf16[2,480,672]{2,1,0:T(8,128)(2,1)S(1)} %gate.2.refs_0_, bf16[672,1536]{1,0:T(8,128)(2,1)} %copy-done.1, bf16[672,1536]{1,0:T(8,128)(2,1)} %copy-done.11), custom_call_target="tpu_custom_call" | custom-call | flops 8000000000 | bytes 1000000 | tf_op jit(solution)/shard_map/down/pallas_call | solution.py:269
  208.3 5.2 %collective-permute-done.16 = bf16[128,1920]{1,0:T(8,128)(2,1)S(1)} collective-permute-done((bf16[128,1920]{1,0:T(8,128)(2,1)S(1)}, bf16[128,1920]{1,0:T(8,128)(2,1)S(1)}, u32[]{:S(2)}, u32[]{:S(2)}) %collective-permute-start.16) | collective-permute-done | bytes 491552 | tf_op jit(solution)/shard_map/ppermute | solution.py:317
  213.5 8.3 %collective-permute-done.17 = bf16[128,1920]{1,0:T(8,128)(2,1)S(1)} collective-permute-done((bf16[128,1920]{1,0:T(8,128)(2,1)S(1)}, bf16[128,1920]{1,0:T(8,128)(2,1)S(1)}, u32[]{:S(2)}, u32[]{:S(2)}) %collective-permute-start.17) | collective-permute-done | bytes 491552 | tf_op jit(solution)/shard_map/ppermute | solution.py:317
  225.1 5.1 %collective-permute-done.20.refs_2_ = bf16[672,2560]{1,0:T(8,128)(2,1)} collective-permute-done((bf16[672,2560]{1,0:T(8,128)(2,1)}, bf16[672,2560]{1,0:T(8,128)(2,1)}, u32[]{:S(2)}, u32[]{:S(2)}) %collective-permute-start.20) | collective-permute-done | bytes 3440672 | tf_op jit(solution)/shard_map/ppermute | solution.py:348
  230.2 5.3 %down.8 = bf16[128,3200]{1,0:T(8,128)(2,1)S(1)} custom-call(bf16[2,160,672]{2,1,0:T(8,128)(2,1)S(1)} %gate.3.refs_0_, bf16[672,2560]{1,0:T(8,128)(2,1)} %collective-permute-done.18.refs_1_, bf16[672,2560]{1,0:T(8,128)(2,1)} %collective-permute-done.20.refs_2_), custom_call_target="tpu_custom_call" | custom-call | flops 4000000000 | bytes 1000000 | tf_op jit(solution)/shard_map/down/pallas_call | solution.py:269
  237.8 9.3 %down.9 = (bf16[128,3200]{1,0:T(8,128)(2,1)S(1)}, bf16[128,3200]{1,0:T(8,128)(2,1)S(1)}, bf16[128,3200]{1,0:T(8,128)(2,1)S(1)}) custom-call(bf16[2,480,672]{2,1,0:T(8,128)(2,1)S(1)} %gate.2.refs_0_, bf16[672,2560]{1,0:T(8,128)(2,1)} %collective-permute-done.18.refs_1_, bf16[672,2560]{1,0:T(8,128)(2,1)} %collective-permute-done.20.refs_2_), custom_call_target="tpu_custom_call" | custom-call | flops 8000000000 | bytes 1000000 | tf_op jit(solution)/shard_map/down/pallas_call | solution.py:269
  250.9 5.6 %collective-permute-done.22.refs_1_ = bf16[672,2048]{1,0:T(8,128)(2,1)S(1)} collective-permute-done((bf16[672,2048]{1,0:T(8,128)(2,1)}, bf16[672,2048]{1,0:T(8,128)(2,1)S(1)}, u32[]{:S(2)}, u32[]{:S(2)}) %collective-permute-start.22) | collective-permute-done | bytes 2752544 | tf_op jit(solution)/shard_map/ppermute | solution.py:345
  262.3 4.3 %down.10 = bf16[128,2560]{1,0:T(8,128)(2,1)S(1)} custom-call(bf16[2,160,672]{2,1,0:T(8,128)(2,1)S(1)} %gate.3.refs_0_, bf16[672,2048]{1,0:T(8,128)(2,1)S(1)} %collective-permute-done.22.refs_1_, bf16[672,2048]{1,0:T(8,128)(2,1)} %collective-permute-done.25.refs_2_), custom_call_target="tpu_custom_call" | custom-call | flops 3000000000 | bytes 1000000 | tf_op jit(solution)/shard_map/down/pallas_call | solution.py:269
  269.4 7.0 %down.11 = (bf16[128,2560]{1,0:T(8,128)(2,1)S(1)}, bf16[128,2560]{1,0:T(8,128)(2,1)S(1)}, bf16[128,2560]{1,0:T(8,128)(2,1)S(1)}) custom-call(bf16[2,480,672]{2,1,0:T(8,128)(2,1)S(1)} %gate.2.refs_0_, bf16[672,2048]{1,0:T(8,128)(2,1)} %copy-done, bf16[672,2048]{1,0:T(8,128)(2,1)} %collective-permute-done.25.refs_2_), custom_call_target="tpu_custom_call" | custom-call | flops 6000000000 | bytes 1000000 | tf_op jit(solution)/shard_map/down/pallas_call | solution.py:269
  278.7 14.7 %all_to_all.15 = bf16[16,8,1920]{2,1,0:T(8,128)(2,1)S(1)} all-to-all(bf16[16,8,1920]{2,1,0:T(8,128)(2,1)S(1)} %fusion), channel_id=1, replica_groups=mesh['xh'=2,'z'=4,'xl'=2,'y'=4,'core'=2] {'xl','y','xh'}, dimensions={0} | all-to-all | bytes 983040 | tf_op jit(solution)/shard_map/all_to_all | solution.py:374
  293.9 12.7 %collective-permute-done.27 = bf16[128,2560]{1,0:T(8,128)(2,1)S(1)} collective-permute-done((bf16[128,2560]{1,0:T(8,128)(2,1)S(1)}, bf16[128,2560]{1,0:T(8,128)(2,1)S(1)}, u32[]{:S(2)}, u32[]{:S(2)}) %collective-permute-start.27) | collective-permute-done | bytes 655392 | tf_op jit(solution)/shard_map/ppermute | solution.py:317
  309.9 6.7 %all-to-all-start.2 = ((bf16[16,8,5760]{2,1,0:T(8,128)(2,1)}), bf16[16,8,5760]{2,1,0:T(8,128)(2,1)S(1)}, u32[]{:S(2)}, u32[]{:S(2)}) async-start(bf16[16,8,5760]{2,1,0:T(8,128)(2,1)} %maximum_bitcast_fusion), calls=%async_computation.2 | async-start | bytes 2949120 | tf_op jit(solution)/shard_map/all_to_all | solution.py:374
  316.7 22.1 %all-to-all-done.2 = bf16[16,8,5760]{2,1,0:T(8,128)(2,1)S(1)} async-done(((bf16[16,8,5760]{2,1,0:T(8,128)(2,1)}), bf16[16,8,5760]{2,1,0:T(8,128)(2,1)S(1)}, u32[]{:S(2)}, u32[]{:S(2)}) %all-to-all-start.2) | async-done | bytes 1474592 | tf_op jit(solution)/shard_map/all_to_all | solution.py:374
  (100 shorter events, 77.5 us)
Async XLA Ops:
  1.9 17.8 %collective-permute-start = (bf16[128,2176]{1,0:T(8,128)(2,1)S(1)}, bf16[128,2176]{1,0:T(8,128)(2,1)S(1)}, u32[]{:S(2)}, u32[]{:S(2)}) collective-permute-start(bf16[128,2176]{1,0:T(8,128)(2,1)S(1)} %pad_maximum_fusion.refs_0_.refs_5_.refs_10_), channel_id=1, source_target_pairs={{0,64},{1,65},{2,66},{3,67},{4,68},{5,69},{6,70},{7,71},{8,72},{9,... | collective-permute-start | bytes 1671176 | tf_op jit(solution)/shard_map/ppermute | solution.py:327
  19.6 30.7 %collective-permute-start.1 = (bf16[208,6144]{1,0:T(8,128)(2,1)}, bf16[208,6144]{1,0:T(8,128)(2,1)}, u32[]{:S(2)}, u32[]{:S(2)}) collective-permute-start(bf16[208,6144]{1,0:T(8,128)(2,1)} %slice.32), channel_id=1, source_target_pairs={{0,8},{1,72},{8,0},{9,64},{64,9},{65,73},{72,1},{73,65},{2,10},{3,... | collective-permute-start | bytes 7667720 | tf_op jit(solution)/shard_map/ppermute | solution.py:345
  19.9 25.9 %collective-permute-start.2 = (bf16[128,2176]{1,0:T(8,128)(2,1)S(1)}, bf16[128,2176]{1,0:T(8,128)(2,1)S(1)}, u32[]{:S(2)}, u32[]{:S(2)}) collective-permute-start(bf16[128,2176]{1,0:T(8,128)(2,1)S(1)} %get-tuple-element.133), channel_id=1, source_target_pairs={{0,16},{16,32},{32,48},{48,0},{1,17},{17,33},{33,49},{49,1},{2,18}... | collective-permute-start | bytes 1671176 | tf_op jit(solution)/shard_map/ppermute | solution.py:317
  21.9 23.9 %collective-permute-start.3 = (bf16[128,2176]{1,0:T(8,128)(2,1)S(1)}, bf16[128,2176]{1,0:T(8,128)(2,1)S(1)}, u32[]{:S(2)}, u32[]{:S(2)}) collective-permute-start(bf16[128,2176]{1,0:T(8,128)(2,1)S(1)} %get-tuple-element.132), channel_id=1, source_target_pairs={{0,32},{16,48},{32,0},{48,16},{1,33},{17,49},{33,1},{49,17},{2,34}... | collective-permute-start | bytes 1671176 | tf_op jit(solution)/shard_map/ppermute | solution.py:317
  23.1 26.1 %collective-permute-start.4 = (bf16[128,2176]{1,0:T(8,128)(2,1)S(1)}, bf16[128,2176]{1,0:T(8,128)(2,1)S(1)}, u32[]{:S(2)}, u32[]{:S(2)}) collective-permute-start(bf16[128,2176]{1,0:T(8,128)(2,1)S(1)} %get-tuple-element.131), channel_id=1, source_target_pairs={{0,48},{16,0},{32,16},{48,32},{1,49},{17,1},{33,17},{49,33},{2,50}... | collective-permute-start | bytes 1671176 | tf_op jit(solution)/shard_map/ppermute | solution.py:317
  50.3 20.4 %collective-permute-start.6 = (bf16[208,6144]{1,0:T(8,128)(2,1)}, bf16[208,6144]{1,0:T(8,128)(2,1)}, u32[]{:S(2)}, u32[]{:S(2)}) collective-permute-start(bf16[208,6144]{1,0:T(8,128)(2,1)} %collective-permute-done.1.refs_6_.refs_2_), channel_id=1, source_target_pairs={{0,1},{1,0},{2,3},{3,2},{4,5},{5,4},{6,7},{7,6},{8,9},{9,8},{10,11... | collective-permute-start | bytes 7667720 | tf_op jit(solution)/shard_map/ppermute | solution.py:348
  50.5 20.2 %collective-permute-start.5 = (bf16[128,6144]{1,0:T(8,128)(2,1)}, bf16[128,6144]{1,0:T(8,128)(2,1)}, u32[]{:S(2)}, u32[]{:S(2)}) collective-permute-start(bf16[128,6144]{1,0:T(8,128)(2,1)} %slice.33), channel_id=1, source_target_pairs={{0,8},{1,72},{8,0},{9,64},{64,9},{65,73},{72,1},{73,65},{2,10},{3,... | collective-permute-start | bytes 4718600 | tf_op jit(solution)/shard_map/ppermute | solution.py:345
  70.7 37.3 %all-to-all-start = ((bf16[16,16,3840]{2,1,0:T(8,128)(2,1)}), bf16[16,16,3840]{2,1,0:T(8,128)(2,1)S(1)}, u32[]{:S(2)}, u32[]{:S(2)}) async-start(bf16[16,16,3840]{2,1,0:T(8,128)(2,1)} %bitcast.43), calls=%async_computation | async-start | bytes 3932160 | tf_op jit(solution)/shard_map/all_to_all | solution.py:374
  108.0 47.4 %collective-permute-start.10 = (bf16[336,6144]{1,0:T(8,128)(2,1)}, bf16[336,6144]{1,0:T(8,128)(2,1)S(1)}, u32[]{:S(2)}, u32[]{:S(2)}) collective-permute-start(bf16[336,6144]{1,0:T(8,128)(2,1)} %slice.37), channel_id=1, source_target_pairs={{0,8},{1,72},{8,0},{9,64},{64,9},{65,73},{72,1},{73,65},{2,10},{3,... | collective-permute-start | bytes 12386312 | tf_op jit(solution)/shard_map/ppermute | solution.py:345
  108.2 45.0 %collective-permute-start.8 = (bf16[256,3840]{1,0:T(8,128)(2,1)S(1)}, bf16[256,3840]{1,0:T(8,128)(2,1)S(1)}, u32[]{:S(2)}, u32[]{:S(2)}) collective-permute-start(bf16[256,3840]{1,0:T(8,128)(2,1)S(1)} %bitcast.39), channel_id=1, source_target_pairs={{0,16},{16,32},{32,48},{48,0},{1,17},{17,33},{33,49},{49,1},{2,18}... | collective-permute-start | bytes 5898248 | tf_op jit(solution)/shard_map/ppermute | solution.py:317
  110.1 44.7 %collective-permute-start.9 = (bf16[256,3840]{1,0:T(8,128)(2,1)S(1)}, bf16[256,3840]{1,0:T(8,128)(2,1)S(1)}, u32[]{:S(2)}, u32[]{:S(2)}) collective-permute-start(bf16[256,3840]{1,0:T(8,128)(2,1)S(1)} %bitcast.40), channel_id=1, source_target_pairs={{0,48},{16,0},{32,16},{48,32},{1,49},{17,1},{33,17},{49,33},{2,50}... | collective-permute-start | bytes 5898248 | tf_op jit(solution)/shard_map/ppermute | solution.py:317
  155.5 27.6 %collective-permute-start.14 = (bf16[672,1536]{1,0:T(8,128)(2,1)S(1)}, bf16[672,1536]{1,0:T(8,128)(2,1)S(1)}, u32[]{:S(2)}, u32[]{:S(2)}) collective-permute-start(bf16[672,1536]{1,0:T(8,128)(2,1)S(1)} %copy-done.5), channel_id=1, source_target_pairs={{0,8},{1,72},{8,0},{9,64},{64,9},{65,73},{72,1},{73,65},{2,10},{3,... | collective-permute-start | bytes 6193160 | tf_op jit(solution)/shard_map/ppermute | solution.py:345
  156.2 24.8 %collective-permute-start.12 = (bf16[128,3840]{1,0:T(8,128)(2,1)S(1)}, bf16[128,3840]{1,0:T(8,128)(2,1)S(1)}, u32[]{:S(2)}, u32[]{:S(2)}) collective-permute-start(bf16[128,3840]{1,0:T(8,128)(2,1)S(1)} %slice.30), channel_id=1, source_target_pairs={{0,16},{16,32},{32,48},{48,0},{1,17},{17,33},{33,49},{49,1},{2,18}... | collective-permute-start | bytes 2949128 | tf_op jit(solution)/shard_map/ppermute | solution.py:317
  159.2 23.9 %collective-permute-start.13 = (bf16[128,3840]{1,0:T(8,128)(2,1)}, bf16[128,3840]{1,0:T(8,128)(2,1)S(1)}, u32[]{:S(2)}, u32[]{:S(2)}) collective-permute-start(bf16[128,3840]{1,0:T(8,128)(2,1)} %slice.31), channel_id=1, source_target_pairs={{0,48},{16,0},{32,16},{48,32},{1,49},{17,1},{33,17},{49,33},{2,50}... | collective-permute-start | bytes 2949128 | tf_op jit(solution)/shard_map/ppermute | solution.py:317
  183.9 40.0 %collective-permute-start.18 = (bf16[672,2560]{1,0:T(8,128)(2,1)S(1)}, bf16[672,2560]{1,0:T(8,128)(2,1)}, u32[]{:S(2)}, u32[]{:S(2)}) collective-permute-start(bf16[672,2560]{1,0:T(8,128)(2,1)S(1)} %copy-done.3), channel_id=1, source_target_pairs={{0,8},{1,72},{8,0},{9,64},{64,9},{65,73},{72,1},{73,65},{2,10},{3,... | collective-permute-start | bytes 10321928 | tf_op jit(solution)/shard_map/ppermute | solution.py:345
  223.8 32.7 %collective-permute-start.22 = (bf16[672,2048]{1,0:T(8,128)(2,1)}, bf16[672,2048]{1,0:T(8,128)(2,1)S(1)}, u32[]{:S(2)}, u32[]{:S(2)}) collective-permute-start(bf16[672,2048]{1,0:T(8,128)(2,1)} %slice.36), channel_id=1, source_target_pairs={{0,8},{1,72},{8,0},{9,64},{64,9},{65,73},{72,1},{73,65},{2,10},{3,... | collective-permute-start | bytes 8257544 | tf_op jit(solution)/shard_map/ppermute | solution.py:345
  235.5 21.0 %collective-permute-start.21 = (bf16[128,3200]{1,0:T(8,128)(2,1)S(1)}, bf16[128,3200]{1,0:T(8,128)(2,1)S(1)}, u32[]{:S(2)}, u32[]{:S(2)}) collective-permute-start(bf16[128,3200]{1,0:T(8,128)(2,1)S(1)} %down.8), channel_id=1, source_target_pairs={{0,48},{16,0},{32,16},{48,32},{1,49},{17,1},{33,17},{49,33},{2,50}... | collective-permute-start | bytes 2457608 | tf_op jit(solution)/shard_map/ppermute | solution.py:317
  236.3 14.6 %collective-permute-start.19 = (bf16[128,1920]{1,0:T(8,128)(2,1)S(1)}, bf16[128,1920]{1,0:T(8,128)(2,1)S(1)}, u32[]{:S(2)}, u32[]{:S(2)}) collective-permute-start(bf16[128,1920]{1,0:T(8,128)(2,1)S(1)} %add_convert_fusion.4), channel_id=1, source_target_pairs={{0,16},{16,32},{32,48},{48,0},{1,17},{17,33},{33,49},{49,1},{2,18}... | collective-permute-start | bytes 1474568 | tf_op jit(solution)/shard_map/ppermute | solution.py:317
  257.6 35.7 %collective-permute-start.23 = (bf16[128,3200]{1,0:T(8,128)(2,1)S(1)}, bf16[128,3200]{1,0:T(8,128)(2,1)S(1)}, u32[]{:S(2)}, u32[]{:S(2)}) collective-permute-start(bf16[128,3200]{1,0:T(8,128)(2,1)S(1)} %add_convert_fusion.1), channel_id=1, source_target_pairs={{0,48},{16,0},{32,16},{48,32},{1,49},{17,1},{33,17},{49,33},{2,50}... | collective-permute-start | bytes 2457608 | tf_op jit(solution)/shard_map/ppermute | solution.py:317
  258.0 35.4 %collective-permute-start.24 = (bf16[128,3200]{1,0:T(8,128)(2,1)S(1)}, bf16[128,3200]{1,0:T(8,128)(2,1)S(1)}, u32[]{:S(2)}, u32[]{:S(2)}) collective-permute-start(bf16[128,3200]{1,0:T(8,128)(2,1)S(1)} %get-tuple-element.115), channel_id=1, source_target_pairs={{0,16},{16,32},{32,48},{48,0},{1,17},{17,33},{33,49},{49,1},{2,18}... | collective-permute-start | bytes 2457608 | tf_op jit(solution)/shard_map/ppermute | solution.py:317
  266.6 27.4 %collective-permute-start.26 = (bf16[128,2560]{1,0:T(8,128)(2,1)S(1)}, bf16[128,2560]{1,0:T(8,128)(2,1)S(1)}, u32[]{:S(2)}, u32[]{:S(2)}) collective-permute-start(bf16[128,2560]{1,0:T(8,128)(2,1)S(1)} %down.10), channel_id=1, source_target_pairs={{0,32},{16,48},{32,0},{48,16},{1,33},{17,49},{33,1},{49,17},{2,34}... | collective-permute-start | bytes 1966088 | tf_op jit(solution)/shard_map/ppermute | solution.py:317
  276.4 30.2 %collective-permute-start.27 = (bf16[128,2560]{1,0:T(8,128)(2,1)S(1)}, bf16[128,2560]{1,0:T(8,128)(2,1)S(1)}, u32[]{:S(2)}, u32[]{:S(2)}) collective-permute-start(bf16[128,2560]{1,0:T(8,128)(2,1)S(1)} %get-tuple-element.118), channel_id=1, source_target_pairs={{0,48},{16,0},{32,16},{48,32},{1,49},{17,1},{33,17},{49,33},{2,50}... | collective-permute-start | bytes 1966088 | tf_op jit(solution)/shard_map/ppermute | solution.py:317
  277.4 30.6 %collective-permute-start.28 = (bf16[128,2560]{1,0:T(8,128)(2,1)S(1)}, bf16[128,2560]{1,0:T(8,128)(2,1)S(1)}, u32[]{:S(2)}, u32[]{:S(2)}) collective-permute-start(bf16[128,2560]{1,0:T(8,128)(2,1)S(1)} %get-tuple-element.119), channel_id=1, source_target_pairs={{0,16},{16,32},{32,48},{48,0},{1,17},{17,33},{33,49},{49,1},{2,18}... | collective-permute-start | bytes 1966088 | tf_op jit(solution)/shard_map/ppermute | solution.py:317
  309.9 28.8 %all-to-all-start.2 = ((bf16[16,8,5760]{2,1,0:T(8,128)(2,1)}), bf16[16,8,5760]{2,1,0:T(8,128)(2,1)S(1)}, u32[]{:S(2)}, u32[]{:S(2)}) async-start(bf16[16,8,5760]{2,1,0:T(8,128)(2,1)} %maximum_bitcast_fusion), calls=%async_computation.2 | async-start | bytes 2949120 | tf_op jit(solution)/shard_map/all_to_all | solution.py:374
  (20 other events, 261.2 us)
